TPU v7x, 32 devices: a whole 2x2x4 slice. The times are simulated.
32 devices in a mesh: ta: 4 (over z), af: 8 (over y, x, core).
Axes of the slice: x: 2, y: 2, z: 4, core: 2. Of those that a mesh axis runs over, the one named last changes fastest.
Arguments:
- velocity: float32 [16, 512, 128, 128], P(None, ('ta', 'af')), may hold values from -14 to 14
- initial_basis: float32 [512, 64], replicated, may hold values from -6 to 6
Outputs:
- core: float32 [16, 128, 64, 128], P('ta', 'af')
All inputs are finite; a program needn't handle non-finite values.
Results may differ from a plain program's by a relative error of at most 0.00017.
Values sent between devices are 32-bit elements; how exact they have to be, the bound alone decides.
No kernel may reach another device: no remote copies, remote signals or barrier semaphores. Data moves between devices by JAX's collectives and lax.ppermute only.
A program may use at most 64 MiB of HBM per device.

v0:
```python
import jax
import jax.numpy as jnp
from jax import lax
from jax.sharding import PartitionSpec as P

ITERS = 3


def orthonormal(product):
    lower = jnp.linalg.cholesky(
        jnp.dot(
            product.T, product, precision=lax.Precision.HIGHEST, preferred_element_type=jnp.float32
        )
    )
    return jax.scipy.linalg.solve_triangular(lower, product.T, lower=True).T


def local(velocity, initial_basis):
    groups_ta = lax.axis_size("ta")
    groups_af = lax.axis_size("af")
    frames, slab_planes, cells_x, cells_y = velocity.shape
    planes_total = initial_basis.shape[0]
    blocked = velocity.reshape(
        groups_ta, frames // groups_ta, slab_planes, groups_af, cells_x // groups_af, cells_y
    )
    blocked = blocked.transpose(0, 3, 1, 2, 4, 5).reshape(
        groups_ta * groups_af, frames // groups_ta, slab_planes, cells_x // groups_af, cells_y
    )
    fibres = lax.all_to_all(blocked, ("ta", "af"), split_axis=0, concat_axis=2, tiled=True)
    fibres = fibres.reshape(frames // groups_ta, planes_total, cells_x // groups_af, cells_y)
    gram_local = jnp.einsum(
        "fzxy,fwxy->zw",
        fibres,
        fibres,
        precision=lax.Precision.HIGHEST,
        preferred_element_type=jnp.float32,
    )
    gram_matrix = lax.psum(gram_local, ("ta", "af"))
    subspace = initial_basis
    for iteration in range(ITERS):
        subspace = orthonormal(
            jnp.dot(
                gram_matrix,
                subspace,
                precision=lax.Precision.HIGHEST,
                preferred_element_type=jnp.float32,
            )
        )
    return jnp.einsum(
        "fzxy,zk->fxky",
        fibres,
        subspace,
        precision=lax.Precision.HIGHEST,
        preferred_element_type=jnp.float32,
    )


def solution(mesh):
    placed = (P(None, ("ta", "af"), None, None), P())
    return jax.shard_map(
        local, mesh=mesh, in_specs=placed, out_specs=P("ta", "af", None, None), check_vma=False
    )
```

profile of v0, /device:TPU:0, one launch (start us, length us, event | category | flops | bytes accessed | tf_op | source)
XLA Modules:
  0.0 630.5 jit_solution(14638823853485210162)
XLA Ops:
  6.5 15.2 %copy.7 = f32[4,4,16,8,16,128]{5,2,4,1,3,0:T(8,128)S(1)} copy(f32[4,4,16,8,16,128]{5,4,3,2,1,0:T(8,128)} %bitcast.74) | data formatting | bytes 33554432 | tf_op jit(solution)/shard_map/reshape | solution.py:23
  21.8 370.5 %all_to_all.15 = f32[32,4,16,16,128]{4,2,3,1,0:T(8,128)} all-to-all(f32[32,4,16,16,128]{4,2,3,1,0:T(8,128)S(1)} %bitcast.73), channel_id=1, replica_groups=mesh['ta'=4,'af'=8] {'ta','af'}, dimensions={0} | all-to-all | bytes 33554432 | tf_op jit(solution)/shard_map/all_to_all | solution.py:29
  392.3 6.7 %copy.8 = f32[1,4,32,16,16,128]{5,3,2,4,1,0:T(8,128)S(1)} copy(f32[1,4,32,16,16,128]{5,3,4,1,2,0:T(8,128)} %bitcast.72) | data formatting | bytes 33554432 | tf_op jit(solution)/shard_map/all_to_all | solution.py:29
  399.1 5.7 copy-done.1
  404.8 28.6 %convolution_bitcast_fusion.1 = f32[512,512]{1,0:T(8,128)} fusion(f32[4,512,16,128]{3,1,2,0:T(8,128)S(1)} %bitcast.70), kind=kOutput, calls=%fused_computation.1 | convolution fusion | flops 25769803776 | bytes 17825792 | tf_op jit(solution)/shard_map/fzxy,fwxy->zw/dot_general | solution.py:31
  433.4 129.6 %all-reduce.2.cloned.1.call-done = f32[512,512]{1,0:T(8,128)} async-done(((f32[512,512]{1,0:T(8,128)}), f32[512,512]{1,0:T(8,128)}) %all-reduce.2.cloned.1.call-update) | async-done | bytes 1048592 | tf_op jit(solution)/shard_map/psum | solution.py:38
  563.0 2.4 fusion.18
  565.7 5.8 cholesky.59
  571.6 0.6 compare_reduce_fusion.2
  572.2 0.7 fusion.5
  572.9 4.9 custom-call.7
  577.8 0.3 fusion.3
  578.1 2.4 fusion.20
  580.8 5.8 cholesky.70
  586.7 0.6 compare_reduce_fusion.1
  587.4 0.7 fusion.6
  588.0 4.9 custom-call.8
  593.3 2.4 fusion.22
  596.0 5.8 cholesky.81
  601.9 0.6 compare_reduce_fusion
  602.5 0.7 fusion.7
  603.2 4.9 custom-call.9
  608.1 0.3 convolution_bitcast_fusion.2
  608.4 15.3 %convolution_bitcast_fusion = f32[4,16,64,128]{3,2,1,0:T(8,128)} fusion(f32[64,512,1,1]{1,0,3,2:T(8,128)S(1)} %convolution_bitcast_fusion.2, f32[4,512,16,128]{3,1,2,0:T(8,128)} %bitcast.71), kind=kOutput, calls=%fused_computation | convolution fusion | flops 3221225472 | bytes 19005440 | tf_op jit(solution)/shard_map/fzxy,zk->fxky/dot_general | solution.py:49
  (18 shorter events, 1.5 us)
Async XLA Ops:
  6.5 556.4 %copy-start = (f32[512,64]{0,1:T(8,128)S(1)}, f32[512,64]{0,1:T(8,128)}, u32[]{:S(2)}) copy-start(f32[512,64]{0,1:T(8,128)} %param.6) | copy-start | bytes 393220
  6.5 556.4 %all-reduce.2.cloned.1.call-start = ((), (), s32[]{:S(2)}) async-start(), calls=%async_computation.1 | async-start | bytes 2097152 | tf_op jit(solution)/shard_map/psum | solution.py:38
  399.0 5.7 copy-start.1
Sparse Core Ops, SparseCore 0:
  433.5 129.4 all-reduce.1
where the time goes:
time: 631 us
  blocking collectives  371 us (59%)
  waiting for transfers between devices  130 us (21%)
  matrix products  52.8 us (8%)
  other arithmetic  36.2 us (6%)
  local copies, waits for them, and re-layouts  27.9 us (4%)
  between operations  13.5 us (2%)
    all_to_all x1, blocking collectives, local(): lax.all_to_all(blocked, ('ta', 'af'), split_axis=0, concat_axis=2, tiled=...  371 us
    psum x1, waiting for transfers between devices, local(): gram_matrix = lax.psum(gram_local, ('ta', 'af'))  130 us
    dot_general x1, matrix products, local(): jnp.einsum('fzxy,fwxy->zw', fibres, fibres, precision=lax.Precision.HIGHE...  28.6 us
    another operation x9, other arithmetic, orthonormal(): jnp.linalg.cholesky(jnp.dot(product.T, product, precision=lax.Precision.H...  19.6 us
    another operation x6, other arithmetic, orthonormal(): return jax.scipy.linalg.solve_triangular(lower, product.T, lower=True).T  16.6 us
    dot_general x1, matrix products, local(): jnp.einsum('fzxy,zk->fxky', fibres, subspace, precision=lax.Precision.HIG...  15.3 us
    reshape x1, local copies, waits for them, and re-layouts, local(): velocity.reshape(groups_ta, frames // groups_ta, slab_planes, groups_af,...  15.2 us
  transfers between devices with their start and end apart: 1, of which 1 were waited for; matrix products, arithmetic and copies ran while one was open for 0% of the time, Pallas kernels for 0%

commit v1 on v0

v1 whole, which is shorter than its diff:
```python
import functools

import jax
import jax.numpy as jnp
from jax import lax
from jax.experimental import pallas as pl
from jax.experimental.pallas import tpu as pltpu
from jax.sharding import PartitionSpec as P

ITERS = 3
HIGHEST = lax.Precision.HIGHEST
VMEM_LIMIT = 48 * 1024 * 1024
PIVOTS = 8


def split(matrix):
    high = matrix.astype(jnp.bfloat16)
    low = (matrix - high.astype(jnp.float32)).astype(jnp.bfloat16)
    return high, low


def nn(left, right, precision=None):
    return lax.dot_general(
        left, right, (((1,), (0,)), ((), ())), precision=precision,
        preferred_element_type=jnp.float32,
    )


def nt(left, right, precision=None):
    return lax.dot_general(
        left, right, (((1,), (1,)), ((), ())), precision=precision,
        preferred_element_type=jnp.float32,
    )


def largest_step(extent, most):
    step = min(extent, most)
    while extent % step:
        step -= 1
    return step


def plane_matrix(block_ref, first, count):
    sources, _, planes, cells_y = block_ref.shape
    return jnp.concatenate(
        [block_ref[:, first + i].reshape(sources * planes, cells_y) for i in range(count)], axis=1
    )


def gram_kernel(block_ref, before_ref, total_ref):
    @pl.when(pl.program_id(0) == 0)
    def _():
        total_ref[...] = before_ref[...]

    high, low = split(plane_matrix(block_ref, 0, block_ref.shape[1]))
    left = jnp.concatenate([high, high], axis=1)
    right = jnp.concatenate([high, low * jnp.bfloat16(2)], axis=1)
    total_ref[...] += nt(left, right)


def gram_add(block, before):
    sources, cells_x, planes, cells_y = block.shape
    planes_total = sources * planes
    step = largest_step(cells_x, 4)
    whole = pl.BlockSpec((planes_total, planes_total), lambda i: (0, 0))
    return pl.pallas_call(
        gram_kernel,
        grid=(cells_x // step,),
        in_specs=[pl.BlockSpec((sources, step, planes, cells_y), lambda i: (0, i, 0, 0)), whole],
        out_specs=whole,
        out_shape=jax.ShapeDtypeStruct((planes_total, planes_total), jnp.float32),
        compiler_params=pltpu.CompilerParams(vmem_limit_bytes=VMEM_LIMIT),
        name="gram_add",
    )(block, before)


def inverse_cholesky(matrix):
    size = matrix.shape[0]
    rows = lax.broadcasted_iota(jnp.int32, (size, 2 * size), 0)
    lanes = lax.broadcasted_iota(jnp.int32, (size, size), 1)
    identity = (lanes == rows[:, :size]).astype(jnp.float32)
    work = jnp.concatenate([matrix, identity], axis=1)
    scale = jnp.zeros_like(work)
    for first in range(0, size, PIVOTS):
        columns = [
            jnp.broadcast_to(work[:, first + i : first + i + 1], work.shape) for i in range(PIVOTS)
        ]
        for i in range(PIVOTS):
            j = first + i
            pivot = columns[i][j : j + 1]
            scale = jnp.where(rows == j, lax.rsqrt(pivot), scale)
            factor = jnp.where(rows > j, columns[i] * (1.0 / pivot), 0.0)
            work = work - factor * work[j : j + 1]
            for m in range(i + 1, PIVOTS):
                columns[m] = columns[m] - factor * columns[m][j : j + 1]
    return (work * scale)[:, size:]


def iterate_kernel(total_ref, basis_ref, out_ref):
    total = total_ref[...]
    gram = 0.5 * (total + total.T)
    subspace = basis_ref[...]
    for _ in range(ITERS):
        product = nn(subspace, gram, HIGHEST)
        inverse = inverse_cholesky(nt(product, product, HIGHEST))
        subspace = nn(inverse, product, HIGHEST)
    out_ref[...] = subspace


def iterate(total, basis_t):
    return pl.pallas_call(
        iterate_kernel,
        out_shape=jax.ShapeDtypeStruct(basis_t.shape, jnp.float32),
        compiler_params=pltpu.CompilerParams(vmem_limit_bytes=VMEM_LIMIT),
        name="iterate",
    )(total, basis_t)


def project_kernel(count, subspace_ref, *refs):
    blocks, out_ref = refs[:count], refs[count]
    rank = subspace_ref.shape[0]
    basis_high, basis_low = split(subspace_ref[...])
    both = jnp.concatenate([basis_high, basis_low], axis=0)
    for j, block_ref in enumerate(blocks):
        step, cells_y = block_ref.shape[1], block_ref.shape[3]
        high, low = split(plane_matrix(block_ref, 0, step))
        main = nn(both, high)
        result = main[:rank] + (main[rank:] + nn(basis_high, low))
        for i in range(step):
            out_ref[j, i] = result[:, i * cells_y : (i + 1) * cells_y]


def project(subspace, blocks):
    sources, cells_x, planes, cells_y = blocks[0].shape
    rank = subspace.shape[0]
    step = largest_step(cells_x, 2)
    return pl.pallas_call(
        functools.partial(project_kernel, len(blocks)),
        grid=(cells_x // step,),
        in_specs=[pl.BlockSpec(subspace.shape, lambda i: (0, 0))]
        + [pl.BlockSpec((sources, step, planes, cells_y), lambda i: (0, i, 0, 0))] * len(blocks),
        out_specs=pl.BlockSpec((len(blocks), step, rank, cells_y), lambda i: (0, i, 0, 0)),
        out_shape=jax.ShapeDtypeStruct((len(blocks), cells_x, rank, cells_y), jnp.float32),
        compiler_params=pltpu.CompilerParams(vmem_limit_bytes=VMEM_LIMIT),
        name="project",
    )(subspace, *blocks)


def sum_over_devices(total):
    groups_af = lax.axis_size("af")
    groups_ta = lax.axis_size("ta")
    rows = total.shape[0] // groups_af
    parts = lax.all_to_all(
        total.reshape(groups_af, rows, total.shape[1]), "af", split_axis=0, concat_axis=0, tiled=True
    )
    mine = parts.sum(axis=0)
    summed = mine
    for distance in range(1, groups_ta):
        summed = summed + lax.ppermute(
            mine, "ta", [(i, (i + distance) % groups_ta) for i in range(groups_ta)]
        )
    spread = jnp.broadcast_to(summed[None], (groups_af,) + summed.shape)
    return lax.all_to_all(spread, "af", split_axis=0, concat_axis=0, tiled=True).reshape(total.shape)


def local(velocity, initial_basis):
    groups_ta = lax.axis_size("ta")
    groups_af = lax.axis_size("af")
    devices = groups_ta * groups_af
    frames, planes, cells_x, cells_y = velocity.shape
    planes_total = initial_basis.shape[0]
    block_frames, block_x = frames // groups_ta, cells_x // groups_af
    split_up = velocity.reshape(groups_ta, block_frames, planes, groups_af, block_x, cells_y)
    blocks = []
    total = jnp.zeros((planes_total, planes_total), jnp.float32)
    for j in range(block_frames):
        outgoing = split_up[:, j].transpose(0, 2, 3, 1, 4)
        outgoing = outgoing.reshape(devices, block_x, planes, cells_y)
        block = lax.all_to_all(outgoing, ("ta", "af"), split_axis=0, concat_axis=0, tiled=True)
        if planes % 8:
            block = block.transpose(1, 0, 2, 3).reshape(1, block_x, planes_total, cells_y)
        blocks.append(block)
        total = gram_add(block, total)
    total = sum_over_devices(total)
    subspace = iterate(total, initial_basis.T)
    return project(subspace, blocks)


def solution(mesh):
    placed = (P(None, ("ta", "af"), None, None), P())
    return jax.shard_map(
        local, mesh=mesh, in_specs=placed, out_specs=P("ta", "af", None, None), check_vma=False
    )
```

time: 631 us -> 485 us (0.77)
  blocking collectives: 371 us -> 36.7 us
  waiting for transfers between devices: 130 us -> 351 us
  matrix products: 52.8 us -> 0 us
  Pallas kernels: 0 us -> 38.5 us
  other arithmetic: 36.2 us -> 0.11 us
  starting transfers between devices: 0.01 us -> 22.4 us
  between operations: 13.5 us -> 0.11 us
  local copies, waits for them, and re-layouts: 27.9 us -> 35.3 us
    all_to_all x0 -> x4, waiting for transfers between devices: none -> 341 us  [local(): lax.all_to_all(outgoing, ('ta', 'af'), split_axis=0, concat_axis=0, tiled...]
    all_to_all x1 -> x2, blocking collectives: 371 us -> 36.7 us  [the longest x1 18.9 us: sum_over_devices(): lax.all_to_all(total.reshape(groups_af, rows, total.shape[1]), 'af', spli...]
    psum x1 -> x0, waiting for transfers between devices: 130 us -> none  [local(): gram_matrix = lax.psum(gram_local, ('ta', 'af'))]
    dot_general x8 -> x0, matrix products: 51.7 us -> none  [the longest x1 28.6 us: local(): jnp.einsum('fzxy,fwxy->zw', fibres, fibres, precision=lax.Precision.HIGHE...]
    pallas_call x0 -> x6, Pallas kernels: none -> 38.5 us  [the longest x4 19.6 us: gram_add(): pl.pallas_call(gram_kernel, grid=(cells_x // step,), in_specs=[pl.BlockSp...]
    another operation x15 -> x0, other arithmetic: 36.2 us -> none  [the longest x9 19.6 us: orthonormal(): jnp.linalg.cholesky(jnp.dot(product.T, product, precision=lax.Precision.H...]
    all_to_all x0 -> x4, starting transfers between devices: none -> 19.9 us  [local(): lax.all_to_all(outgoing, ('ta', 'af'), split_axis=0, concat_axis=0, tiled...]
    unnamed x4 -> x6, local copies, waits for them, and re-layouts: 5.71 us -> 24.1 us
  transfers between devices with their start and end apart: 1 -> 7, of which waited for: 1 -> 6; matrix products, arithmetic and copies ran while one was open for 0% -> 4% of each run, Pallas kernels for 0% -> 3%
where the time goes in v1:
time: 485 us; the launch traced here: 484 us
  waiting for transfers between devices  351 us (72%)
  Pallas kernels  38.5 us (8%)
  blocking collectives  36.7 us (8%)
  local copies, waits for them, and re-layouts  35.3 us (7%)
  starting transfers between devices  22.4 us (5%)
    all_to_all x4, waiting for transfers between devices, local(): lax.all_to_all(outgoing, ('ta', 'af'), split_axis=0, concat_axis=0, tiled...  341 us
    unnamed x6, local copies, waits for them, and re-layouts  24.1 us
    all_to_all x4, starting transfers between devices, local(): lax.all_to_all(outgoing, ('ta', 'af'), split_axis=0, concat_axis=0, tiled...  19.9 us
    pallas_call x4, Pallas kernels, gram_add(): pl.pallas_call(gram_kernel, grid=(cells_x // step,), in_specs=[pl.BlockSp...  19.6 us
    all_to_all x1, blocking collectives, sum_over_devices(): lax.all_to_all(total.reshape(groups_af, rows, total.shape[1]), 'af', spli...  18.9 us
    all_to_all x1, blocking collectives, sum_over_devices(): lax.all_to_all(spread, 'af', split_axis=0, concat_axis=0, tiled=True)  17.8 us
    slice x1, local copies, waits for them, and re-layouts, local(): outgoing = split_up[:, j].transpose(0, 2, 3, 1, 4)  11 us
    pallas_call x1, Pallas kernels, project(): pl.pallas_call(functools.partial(project_kernel, len(blocks)), grid=(cell...  10.2 us
  transfers between devices with their start and end apart: 7, of which 6 were waited for; matrix products, arithmetic and copies ran while one was open for 4% of the time, Pallas kernels for 3%

profile of v1, /device:TPU:0, one launch (start us, length us, event | category | flops | bytes accessed | tf_op | source)
XLA Modules:
  0.0 483.9 jit_solution(11867821504789805397)
XLA Ops:
  0.0 11.0 %fusion = (f32[4,1,16,8,16,128]{5,4,3,2,1,0:T(8,128)}, f32[4,1,16,8,16,128]{5,4,3,2,1,0:T(8,128)}, f32[4,1,16,8,16,128]{5,4,3,2,1,0:T(8,128)S(1)}, f32[4,1,16,8,16,128]{5,4,3,2,1,0:T(8,128)}) fusion(f32[4,4,16,8,16,128]{5,4,3,2,1,0:T(8,128)} %bitcast.27), kind=kLoop, calls=%fused_computation.1 | loop fusion | bytes 33554432 | tf_op jit(solution)/shard_map/slice | solution.py:177
  11.0 4.4 copy.8
  15.4 7.4 %all-to-all-start.1 = ((f32[32,16,16,128]{3,2,1,0:T(8,128)}), f32[32,16,16,128]{3,2,1,0:T(8,128)}, u32[]{:S(2)}, u32[]{:S(2)}) async-start(f32[32,16,16,128]{3,2,1,0:T(8,128)} %bitcast.31), calls=%async_computation.1 | async-start | bytes 8388608 | tf_op jit(solution)/shard_map/all_to_all | solution.py:179
  22.8 6.6 %copy.9 = f32[4,1,16,8,16,128]{5,2,4,3,0,1:T(8,128)} copy(f32[4,1,16,8,16,128]{5,4,3,2,1,0:T(8,128)} %get-tuple-element.6) | data formatting | bytes 8388608
  29.4 87.3 %all-to-all-done.1.block_ref.refs_2_ = f32[32,16,16,128]{3,2,1,0:T(8,128)} async-done(((f32[32,16,16,128]{3,2,1,0:T(8,128)}), f32[32,16,16,128]{3,2,1,0:T(8,128)}, u32[]{:S(2)}, u32[]{:S(2)}) %all-to-all-start.1) | async-done | bytes 4194336 | tf_op jit(solution)/shard_map/all_to_all | solution.py:179
  116.7 4.1 all-to-all-start.2
  120.8 6.6 %copy.10 = f32[4,1,16,8,16,128]{5,2,4,3,0,1:T(8,128)} copy(f32[4,1,16,8,16,128]{5,4,3,2,1,0:T(8,128)} %get-tuple-element.5) | data formatting | bytes 8388608
  127.4 87.3 %all-to-all-done.2.block_ref.refs_1_ = f32[32,16,16,128]{3,2,1,0:T(8,128)} async-done(((f32[32,16,16,128]{3,2,1,0:T(8,128)}), f32[32,16,16,128]{3,2,1,0:T(8,128)}, u32[]{:S(2)}, u32[]{:S(2)}) %all-to-all-start.2) | async-done | bytes 4194336 | tf_op jit(solution)/shard_map/all_to_all | solution.py:179
  214.7 4.1 all-to-all-start.3
  218.8 6.6 %copy.7 = f32[4,1,16,8,16,128]{5,2,4,3,0,1:T(8,128)} copy(f32[4,1,16,8,16,128]{5,4,3,2,1,0:T(8,128)} %get-tuple-element.8) | data formatting | bytes 8388608
  225.3 87.3 %all-to-all-done.3.block_ref.refs_0_ = f32[32,16,16,128]{3,2,1,0:T(8,128)} async-done(((f32[32,16,16,128]{3,2,1,0:T(8,128)}), f32[32,16,16,128]{3,2,1,0:T(8,128)}, u32[]{:S(2)}, u32[]{:S(2)}) %all-to-all-start.3) | async-done | bytes 4194336 | tf_op jit(solution)/shard_map/all_to_all | solution.py:179
  312.6 4.3 all-to-all-start
  317.0 4.9 %gram_add.4.before_ref = f32[512,512]{1,0:T(8,128)S(1)} custom-call(f32[32,16,16,128]{3,2,1,0:T(8,128)} %all-to-all-done.3.block_ref.refs_0_, f32[512,512]{1,0:T(8,128)S(1)} %broadcast_in_dim.4.before_ref), custom_call_target="tpu_custom_call" | custom-call | tf_op jit(solution)/shard_map/gram_add/pallas_call | solution.py:66
  322.0 4.9 %gram_add.5.before_ref = f32[512,512]{1,0:T(8,128)S(1)} custom-call(f32[32,16,16,128]{3,2,1,0:T(8,128)} %all-to-all-done.2.block_ref.refs_1_, f32[512,512]{1,0:T(8,128)S(1)} %gram_add.4.before_ref), custom_call_target="tpu_custom_call" | custom-call | tf_op jit(solution)/shard_map/gram_add/pallas_call | solution.py:66
  326.9 4.9 %gram_add.6.before_ref = f32[512,512]{1,0:T(8,128)S(1)} custom-call(f32[32,16,16,128]{3,2,1,0:T(8,128)} %all-to-all-done.1.block_ref.refs_2_, f32[512,512]{1,0:T(8,128)S(1)} %gram_add.5.before_ref), custom_call_target="tpu_custom_call" | custom-call | tf_op jit(solution)/shard_map/gram_add/pallas_call | solution.py:66
  331.8 78.9 %all-to-all-done.block_ref.refs_3_ = f32[32,16,16,128]{3,2,1,0:T(8,128)} async-done(((f32[32,16,16,128]{3,2,1,0:T(8,128)}), f32[32,16,16,128]{3,2,1,0:T(8,128)}, u32[]{:S(2)}, u32[]{:S(2)}) %all-to-all-start) | async-done | bytes 4194336 | tf_op jit(solution)/shard_map/all_to_all | solution.py:179
  410.7 4.9 %gram_add.7 = f32[512,512]{1,0:T(8,128)S(1)} custom-call(f32[32,16,16,128]{3,2,1,0:T(8,128)} %all-to-all-done.block_ref.refs_3_, f32[512,512]{1,0:T(8,128)S(1)} %gram_add.6.before_ref), custom_call_target="tpu_custom_call" | custom-call | tf_op jit(solution)/shard_map/gram_add/pallas_call | solution.py:66
  415.6 18.9 %all_to_all.30 = f32[8,64,512]{2,1,0:T(8,128)S(1)} all-to-all(f32[8,64,512]{2,1,0:T(8,128)S(1)} %bitcast.25), channel_id=1, replica_groups=mesh['ta'=4,'af'=8] {'af'}, dimensions={0} | all-to-all | bytes 2097152 | tf_op jit(solution)/shard_map/all_to_all | solution.py:153
  434.6 1.8 collective-permute-start.2
  437.0 3.3 collective-permute-done.2
  440.4 6.7 %collective-permute-done.1 = f32[64,512]{1,0:T(8,128)S(1)} collective-permute-done((f32[64,512]{1,0:T(8,128)S(1)}, f32[64,512]{1,0:T(8,128)S(1)}, u32[]{:S(2)}, u32[]{:S(2)}) %collective-permute-start.1) | collective-permute-done | bytes 131104 | tf_op jit(solution)/shard_map/ppermute | solution.py:159
  447.2 17.8 %all_to_all.31 = f32[8,64,512]{2,1,0:T(8,128)S(1)} all-to-all(f32[8,64,512]{2,1,0:T(8,128)S(1)} %broadcast_in_dim.10), channel_id=1, replica_groups=mesh['ta'=4,'af'=8] {'af'}, dimensions={0} | all-to-all | bytes 2097152 | tf_op jit(solution)/shard_map/all_to_all | solution.py:163
  465.0 8.7 %iterate.1.subspace_ref = f32[64,512]{1,0:T(8,128)S(1)} custom-call(f32[512,512]{1,0:T(8,128)S(1)} %bitcast.24, f32[64,512]{1,0:T(8,128)S(1)} %bitcast.26), custom_call_target="tpu_custom_call" | custom-call | tf_op jit(solution)/shard_map/iterate/pallas_call | solution.py:111
  473.7 10.2 %project.1 = f32[4,16,64,128]{3,2,1,0:T(8,128)} custom-call(f32[64,512]{1,0:T(8,128)S(1)} %iterate.1.subspace_ref, f32[32,16,16,128]{3,2,1,0:T(8,128)} %all-to-all-done.3.block_ref.refs_0_, f32[32,16,16,128]{3,2,1,0:T(8,128)} %all-to-all-done.2.block_ref.refs_1_, f32[32,16,16,128]{3,2,1,0:T(8,128)} %all-to-all-done.1.block_ref.refs_2_, ...), custom_call_target="tpu_custom_call" | custom-call | tf_op jit(solution)/shard_map/project/pallas_call | solution.py:137
  (9 shorter events, 1.0 us)
Async XLA Ops:
  15.4 101.3 %all-to-all-start.1 = ((f32[32,16,16,128]{3,2,1,0:T(8,128)}), f32[32,16,16,128]{3,2,1,0:T(8,128)}, u32[]{:S(2)}, u32[]{:S(2)}) async-start(f32[32,16,16,128]{3,2,1,0:T(8,128)} %bitcast.31), calls=%async_computation.1 | async-start | bytes 8388608 | tf_op jit(solution)/shard_map/all_to_all | solution.py:179
  116.7 98.0 %all-to-all-start.2 = ((f32[32,16,16,128]{3,2,1,0:T(8,128)}), f32[32,16,16,128]{3,2,1,0:T(8,128)}, u32[]{:S(2)}, u32[]{:S(2)}) async-start(f32[32,16,16,128]{3,2,1,0:T(8,128)} %bitcast.30), calls=%async_computation.2 | async-start | bytes 8388608 | tf_op jit(solution)/shard_map/all_to_all | solution.py:179
  214.7 98.0 %all-to-all-start.3 = ((f32[32,16,16,128]{3,2,1,0:T(8,128)}), f32[32,16,16,128]{3,2,1,0:T(8,128)}, u32[]{:S(2)}, u32[]{:S(2)}) async-start(f32[32,16,16,128]{3,2,1,0:T(8,128)} %bitcast.29), calls=%async_computation.3 | async-start | bytes 8388608 | tf_op jit(solution)/shard_map/all_to_all | solution.py:179
  312.6 98.1 %all-to-all-start = ((f32[32,16,16,128]{3,2,1,0:T(8,128)}), f32[32,16,16,128]{3,2,1,0:T(8,128)}, u32[]{:S(2)}, u32[]{:S(2)}) async-start(f32[32,16,16,128]{3,2,1,0:T(8,128)} %bitcast.28), calls=%async_computation | async-start | bytes 8388608 | tf_op jit(solution)/shard_map/all_to_all | solution.py:179
  415.6 49.4 %copy-start = (f32[512,64]{0,1:T(8,128)S(1)}, f32[512,64]{0,1:T(8,128)}, u32[]{:S(2)}) copy-start(f32[512,64]{0,1:T(8,128)} %param.3) | copy-start | bytes 393220
  434.6 5.8 %collective-permute-start.2 = (f32[64,512]{1,0:T(8,128)S(1)}, f32[64,512]{1,0:T(8,128)S(1)}, u32[]{:S(2)}, u32[]{:S(2)}) collective-permute-start(f32[64,512]{1,0:T(8,128)S(1)} %reduce_sum.9), channel_id=1, source_target_pairs={{0,24},{8,0},{16,8},{24,16},{1,25},{9,1},{17,9},{25,17},{2,26},{10... | collective-permute-start | bytes 393224 | tf_op jit(solution)/shard_map/ppermute | solution.py:159
  436.4 10.6 %collective-permute-start.1 = (f32[64,512]{1,0:T(8,128)S(1)}, f32[64,512]{1,0:T(8,128)S(1)}, u32[]{:S(2)}, u32[]{:S(2)}) collective-permute-start(f32[64,512]{1,0:T(8,128)S(1)} %reduce_sum.9), channel_id=1, source_target_pairs={{0,16},{8,24},{16,0},{24,8},{1,17},{9,25},{17,1},{25,9},{2,18},{10... | collective-permute-start | bytes 393224 | tf_op jit(solution)/shard_map/ppermute | solution.py:159
  436.4 10.6 %collective-permute-start = (f32[64,512]{1,0:T(8,128)S(1)}, f32[64,512]{1,0:T(8,128)S(1)}, u32[]{:S(2)}, u32[]{:S(2)}) collective-permute-start(f32[64,512]{1,0:T(8,128)S(1)} %reduce_sum.9), channel_id=1, source_target_pairs={{0,8},{8,16},{16,24},{24,0},{1,9},{9,17},{17,25},{25,1},{2,10},{10... | collective-permute-start | bytes 393224 | tf_op jit(solution)/shard_map/ppermute | solution.py:159

commit v2 on v1

v2 whole, which is shorter than its diff:
```python
import functools
import math

import jax
import jax.numpy as jnp
from jax import lax
from jax.experimental import pallas as pl
from jax.experimental.pallas import tpu as pltpu
from jax.sharding import PartitionSpec as P

ITERS = 3
HIGHEST = lax.Precision.HIGHEST
VMEM_LIMIT = 48 * 1024 * 1024
PIVOTS = 8
GRAM_CELLS = 4
PROJECT_CELLS = 8


def split(matrix):
    high = matrix.astype(jnp.bfloat16)
    low = (matrix - high.astype(jnp.float32)).astype(jnp.bfloat16)
    return high, low


def nn(left, right, precision=None):
    return lax.dot_general(
        left, right, (((1,), (0,)), ((), ())), precision=precision,
        preferred_element_type=jnp.float32,
    )


def nt(left, right, precision=None):
    return lax.dot_general(
        left, right, (((1,), (1,)), ((), ())), precision=precision,
        preferred_element_type=jnp.float32,
    )


def largest_step(extent, most):
    step = min(extent, most)
    while extent % step:
        step -= 1
    return step


def cell_matrix(block_ref):
    sources, cells, planes, cells_y = block_ref.shape
    return jnp.concatenate(
        [block_ref[:, i].reshape(sources * planes, cells_y) for i in range(cells)], axis=1
    )


def add_products(block_ref, total_ref):
    high, low = split(cell_matrix(block_ref))
    left = jnp.concatenate([high, high], axis=1)
    right = jnp.concatenate([high, low * jnp.bfloat16(2)], axis=1)
    total_ref[...] += nt(left, right)


def gram_kernel(block_ref, total_ref):
    @pl.when(pl.program_id(0) == 0)
    def _():
        total_ref[...] = jnp.zeros_like(total_ref)

    add_products(block_ref, total_ref)


def gram_more_kernel(block_ref, before_ref, total_ref):
    @pl.when(pl.program_id(0) == 0)
    def _():
        total_ref[...] = before_ref[...]

    add_products(block_ref, total_ref)


def lower_blocks(count):
    return [(i, j) for i in range(count) for j in range(i + 1)]


def gram_pack_kernel(block_ref, before_ref, packed_ref, total_ref):
    gram_more_kernel(block_ref, before_ref, total_ref)

    @pl.when(pl.program_id(0) == pl.num_programs(0) - 1)
    def _():
        group = packed_ref.shape[1]
        blocks = lower_blocks(total_ref.shape[0] // group)
        for n, (i, j) in enumerate(blocks):
            block = total_ref[i * group : (i + 1) * group, j * group : (j + 1) * group]
            mirrored = total_ref[j * group : (j + 1) * group, i * group : (i + 1) * group]
            packed_ref[n * group : (n + 1) * group, :] = 0.5 * (block + mirrored.T)
        rest = packed_ref.shape[0] - len(blocks) * group
        if rest:
            packed_ref[len(blocks) * group :, :] = jnp.zeros((rest, group), jnp.float32)


def gram(block, before, parts=None):
    sources, cells, planes, cells_y = block.shape
    planes_total = sources * planes
    step = largest_step(cells, GRAM_CELLS)
    square = (planes_total, planes_total)
    whole = pl.BlockSpec(square, lambda i: (0, 0))
    in_specs = [pl.BlockSpec((sources, step, planes, cells_y), lambda i: (0, i, 0, 0))]
    operands = [block]
    kernel, out_shape, scratch = gram_kernel, square, []
    if before is not None:
        in_specs.append(whole)
        operands.append(before)
        kernel = gram_more_kernel
    if parts is not None:
        group = planes_total // largest_step(planes_total, planes_total // 128)
        rows = len(lower_blocks(planes_total // group)) * group
        out_shape = (rows + -rows % (8 * parts), group)
        kernel, scratch = gram_pack_kernel, [pltpu.VMEM(square, jnp.float32)]
    return pl.pallas_call(
        kernel,
        grid=(cells // step,),
        in_specs=in_specs,
        out_specs=pl.BlockSpec(out_shape, lambda i: (0, 0)),
        out_shape=jax.ShapeDtypeStruct(out_shape, jnp.float32),
        scratch_shapes=scratch,
        compiler_params=pltpu.CompilerParams(vmem_limit_bytes=VMEM_LIMIT),
        name="gram",
    )(*operands)


def inverse_cholesky(matrix):
    size = matrix.shape[0]
    rows = lax.broadcasted_iota(jnp.int32, (size, 2 * size), 0)
    lanes = lax.broadcasted_iota(jnp.int32, (size, size), 1)
    identity = (lanes == rows[:, :size]).astype(jnp.float32)
    work = jnp.concatenate([matrix, identity], axis=1)
    scale = jnp.zeros_like(work)
    for first in range(0, size, PIVOTS):
        columns = [
            jnp.broadcast_to(work[:, first + i : first + i + 1], work.shape) for i in range(PIVOTS)
        ]
        for i in range(PIVOTS):
            j = first + i
            pivot = columns[i][j : j + 1]
            scale = jnp.where(rows == j, lax.rsqrt(pivot), scale)
            factor = jnp.where(rows > j, columns[i] * (1.0 / pivot), 0.0)
            work = work - factor * work[j : j + 1]
            for m in range(i + 1, PIVOTS):
                columns[m] = columns[m] - factor * columns[m][j : j + 1]
    return (work * scale)[:, size:]


def iterate_kernel(packed_ref, basis_ref, out_ref, gram_ref):
    group = packed_ref.shape[1]
    for n, (i, j) in enumerate(lower_blocks(gram_ref.shape[0] // group)):
        block = packed_ref[n * group : (n + 1) * group, :]
        gram_ref[i * group : (i + 1) * group, j * group : (j + 1) * group] = block
        if i != j:
            gram_ref[j * group : (j + 1) * group, i * group : (i + 1) * group] = block.T
    matrix = gram_ref[...]
    subspace = basis_ref[...]
    for _ in range(ITERS):
        product = nn(subspace, matrix, HIGHEST)
        inverse = inverse_cholesky(nt(product, product, HIGHEST))
        subspace = nn(inverse, product, HIGHEST)
    out_ref[...] = subspace


def iterate(packed, basis_t):
    planes_total = basis_t.shape[1]
    return pl.pallas_call(
        iterate_kernel,
        out_shape=jax.ShapeDtypeStruct(basis_t.shape, jnp.float32),
        scratch_shapes=[pltpu.VMEM((planes_total, planes_total), jnp.float32)],
        compiler_params=pltpu.CompilerParams(vmem_limit_bytes=VMEM_LIMIT),
        name="iterate",
    )(packed, basis_t)


def project_kernel(steps, subspace_ref, *refs):
    blocks, out_ref = refs[:-1], refs[-1]
    rank = subspace_ref.shape[0]
    basis_high, basis_low = split(subspace_ref[...])
    both = jnp.concatenate([basis_high, basis_low], axis=0)
    first = 0
    for count, block_ref in zip(steps, blocks):

        @pl.when((pl.program_id(0) >= first) & (pl.program_id(0) < first + count))
        def _(block_ref=block_ref):
            cells, cells_y = block_ref.shape[1], block_ref.shape[3]
            high, low = split(cell_matrix(block_ref))
            main = nn(both, high)
            result = main[:rank] + (main[rank:] + nn(basis_high, low))
            for i in range(cells):
                out_ref[i] = result[:, i * cells_y : (i + 1) * cells_y]

        first += count


def project(subspace, blocks):
    sources, _, planes, cells_y = blocks[0].shape
    rank = subspace.shape[0]
    cells = [block.shape[1] for block in blocks]
    step = largest_step(math.gcd(*cells), PROJECT_CELLS)
    steps = [count // step for count in cells]
    in_specs = [pl.BlockSpec(subspace.shape, lambda i: (0, 0))]
    for n, count in enumerate(steps):
        first = sum(steps[:n])
        in_specs.append(
            pl.BlockSpec(
                (sources, step, planes, cells_y),
                lambda i, first=first, count=count: (0, jnp.clip(i - first, 0, count - 1), 0, 0),
            )
        )
    return pl.pallas_call(
        functools.partial(project_kernel, steps),
        grid=(sum(steps),),
        in_specs=in_specs,
        out_specs=pl.BlockSpec((step, rank, cells_y), lambda i: (i, 0, 0)),
        out_shape=jax.ShapeDtypeStruct((sum(cells), rank, cells_y), jnp.float32),
        compiler_params=pltpu.CompilerParams(vmem_limit_bytes=VMEM_LIMIT),
        name="project",
    )(subspace, *blocks)


def sum_over_devices(packed):
    groups_af, groups_ta = lax.axis_size("af"), lax.axis_size("ta")
    rows = packed.shape[0] // groups_af
    parts = lax.all_to_all(
        packed.reshape(groups_af, rows, packed.shape[1]), "af", split_axis=0, concat_axis=0, tiled=True
    )
    mine = parts.sum(axis=0)
    summed = mine
    for distance in range(1, groups_ta):
        summed = summed + lax.ppermute(
            mine, "ta", [(i, (i + distance) % groups_ta) for i in range(groups_ta)]
        )
    spread = jnp.broadcast_to(summed[None], (groups_af,) + summed.shape)
    return lax.all_to_all(spread, "af", split_axis=0, concat_axis=0, tiled=True).reshape(packed.shape)


def arrange_kernel(in_ref, out_ref):
    for x in range(in_ref.shape[3]):
        for target in range(in_ref.shape[2]):
            out_ref[target, x] = in_ref[0, :, target, x]


def outgoing(velocity, first, count):
    groups_ta, groups_af = lax.axis_size("ta"), lax.axis_size("af")
    frames, planes, cells_x, cells_y = velocity.shape
    block_frames, block_x = frames // groups_ta, cells_x // groups_af
    part = cell_step(block_x)
    if planes % 8 or part % 8:
        ordered = velocity.reshape(groups_ta, block_frames, planes, groups_af, block_x, cells_y)
        ordered = ordered.transpose(0, 3, 1, 4, 2, 5)
        ordered = ordered.reshape(groups_ta * groups_af, -1, planes, cells_y)
        return ordered[:, first : first + count]
    parts_x, start = block_x // part, first // part

    def source(group, i):
        frame = group * block_frames + (start + i) // parts_x
        return frame, 0, 0, lax.rem(start + i, parts_x), 0

    return pl.pallas_call(
        arrange_kernel,
        grid=(groups_ta, count // part),
        in_specs=[pl.BlockSpec((1, planes, groups_af, part, cells_y), source)],
        out_specs=pl.BlockSpec((groups_af, part, planes, cells_y), lambda group, i: (group, i, 0, 0)),
        out_shape=jax.ShapeDtypeStruct(
            (groups_ta * groups_af, count, planes, cells_y), jnp.float32
        ),
        compiler_params=pltpu.CompilerParams(vmem_limit_bytes=VMEM_LIMIT),
        name="arrange",
    )(velocity.reshape(frames, planes, groups_af, block_x, cells_y))


def cell_step(block_x):
    return 8 if block_x % 8 == 0 else block_x


def local(velocity, initial_basis):
    groups_ta, groups_af = lax.axis_size("ta"), lax.axis_size("af")
    frames, planes, cells_x, cells_y = velocity.shape
    block_frames, block_x = frames // groups_ta, cells_x // groups_af
    cells, part = block_frames * block_x, cell_step(block_x)
    edge = min(part, cells // 3)
    blocks = []
    for first, count in ((0, edge), (edge, cells - 2 * edge), (cells - edge, edge)):
        block = outgoing(velocity, first, count)
        if blocks:
            block, blocks[-1] = lax.optimization_barrier((block, blocks[-1]))
        block = lax.all_to_all(block, ("ta", "af"), split_axis=0, concat_axis=0, tiled=True)
        blocks.append(block)
    if planes % 8:
        blocks = [
            block.transpose(1, 0, 2, 3).reshape(1, block.shape[1], -1, cells_y) for block in blocks
        ]
    total = gram(blocks[0], None)
    total = gram(blocks[1], total)
    packed = sum_over_devices(gram(blocks[2], total, groups_af))
    subspace = iterate(packed, initial_basis.T)
    core = project(subspace, blocks)
    return core.reshape(block_frames, block_x, core.shape[1], cells_y)


def solution(mesh):
    placed = (P(None, ("ta", "af"), None, None), P())
    return jax.shard_map(
        local, mesh=mesh, in_specs=placed, out_specs=P("ta", "af", None, None), check_vma=False
    )
```

time: 485 us -> 457 us (0.942)
  local copies, waits for them, and re-layouts: 35.3 us -> 2.68 us
  Pallas kernels: 38.5 us -> 63.5 us
  blocking collectives: 36.7 us -> 28.1 us
  waiting for transfers between devices: 351 us -> 343 us
    pallas_call x5 -> x7, Pallas kernels: 29.9 us -> 54.9 us  [the longest x3 26 us: outgoing(): pl.pallas_call(arrange_kernel, grid=(groups_ta, count // part), in_specs=...]
    unnamed x6, local copies, waits for them, and re-layouts: 24.1 us -> 2.63 us
    slice x1 -> x0, local copies, waits for them, and re-layouts: 11 us -> none  [local(): outgoing = split_up[:, j].transpose(0, 2, 3, 1, 4)]
    all_to_all x4 -> x3, starting transfers between devices: 19.9 us -> 14.9 us  [local(): lax.all_to_all(block, ('ta', 'af'), split_axis=0, concat_axis=0, tiled=True)]
    all_to_all x4 -> x3, waiting for transfers between devices: 341 us -> 337 us  [local(): lax.all_to_all(block, ('ta', 'af'), split_axis=0, concat_axis=0, tiled=True)]
  transfers between devices with their start and end apart: 7 -> 6, of which waited for: 6 -> 5; matrix products, arithmetic and copies ran while one was open for 4% -> 0% of each run, Pallas kernels for 3% -> 8%
where the time goes in v2:
time: 457 us; the launch traced here: 456 us
  waiting for transfers between devices  343 us (75%)
  Pallas kernels  63.5 us (14%)
  blocking collectives  28.1 us (6%)
  starting transfers between devices  18.8 us (4%)
    all_to_all x3, waiting for transfers between devices, local(): lax.all_to_all(block, ('ta', 'af'), split_axis=0, concat_axis=0, tiled=True)  337 us
    pallas_call x3, Pallas kernels, outgoing(): pl.pallas_call(arrange_kernel, grid=(groups_ta, count // part), in_specs=...  26 us
    pallas_call x3, Pallas kernels, gram(): pl.pallas_call(kernel, grid=(cells // step,), in_specs=in_specs, out_spec...  18 us
    all_to_all x3, starting transfers between devices, local(): lax.all_to_all(block, ('ta', 'af'), split_axis=0, concat_axis=0, tiled=True)  14.9 us
    all_to_all x1, blocking collectives, sum_over_devices(): lax.all_to_all(packed.reshape(groups_af, rows, packed.shape[1]), 'af', sp...  14.5 us
    all_to_all x1, blocking collectives, sum_over_devices(): lax.all_to_all(spread, 'af', split_axis=0, concat_axis=0, tiled=True)  13.5 us
    pallas_call x1, Pallas kernels, project(): pl.pallas_call(functools.partial(project_kernel, steps), grid=(sum(steps)...  10.9 us
  transfers between devices with their start and end apart: 6, of which 5 were waited for; matrix products, arithmetic and copies ran while one was open for 0% of the time, Pallas kernels for 8%

profile of v2, /device:TPU:0, one launch (start us, length us, event | category | flops | bytes accessed | tf_op | source)
XLA Modules:
  0.0 456.0 jit_solution(3090349389664993060)
XLA Ops:
  0.0 3.0 arrange.5
  3.0 0.0 copy-start.1
  3.0 1.3 copy-done.1
  4.3 7.3 %all-to-all-start = ((f32[32,8,16,128]{3,2,1,0:T(8,128)}), f32[32,8,16,128]{3,2,1,0:T(8,128)S(1)}, u32[]{:S(2)}, u32[]{:S(2)}) async-start(f32[32,8,16,128]{3,2,1,0:T(8,128)} %copy-done.1), calls=%async_computation | async-start | bytes 4194304 | tf_op jit(solution)/shard_map/all_to_all | solution.py:287
  11.6 20.0 %arrange.4 = f32[32,48,16,128]{3,2,1,0:T(8,128)} custom-call(f32[16,16,8,16,128]{4,3,2,1,0:T(8,128)} %bitcast.9), custom_call_target="tpu_custom_call" | custom-call | tf_op jit(solution)/shard_map/arrange/pallas_call | solution.py:259
  31.6 28.9 %all-to-all-done.block_ref.refs_0_ = f32[32,8,16,128]{3,2,1,0:T(8,128)S(1)} async-done(((f32[32,8,16,128]{3,2,1,0:T(8,128)}), f32[32,8,16,128]{3,2,1,0:T(8,128)S(1)}, u32[]{:S(2)}, u32[]{:S(2)}) %all-to-all-start) | async-done | bytes 2097184 | tf_op jit(solution)/shard_map/all_to_all | solution.py:287
  60.5 4.1 all-to-all-start.1
  64.6 3.0 arrange.3
  67.7 1.3 copy-done
  69.0 274.4 %all-to-all-done.1.block_ref.refs_1_ = f32[32,48,16,128]{3,2,1,0:T(8,128)} async-done(((f32[32,48,16,128]{3,2,1,0:T(8,128)}), f32[32,48,16,128]{3,2,1,0:T(8,128)}, u32[]{:S(2)}, u32[]{:S(2)}) %all-to-all-start.1) | async-done | bytes 12582944 | tf_op jit(solution)/shard_map/all_to_all | solution.py:287
  343.4 3.5 all-to-all-start.2
  346.9 1.8 gram.3.before_ref
  348.6 13.2 %gram.4.before_ref = f32[512,512]{1,0:T(8,128)S(1)} custom-call(f32[32,48,16,128]{3,2,1,0:T(8,128)} %all-to-all-done.1.block_ref.refs_1_, f32[512,512]{1,0:T(8,128)S(1)} %gram.3.before_ref), custom_call_target="tpu_custom_call" | custom-call | tf_op jit(solution)/shard_map/gram/pallas_call | solution.py:114
  361.8 34.0 %all-to-all-done.2.block_ref.refs_2_ = f32[32,8,16,128]{3,2,1,0:T(8,128)} async-done(((f32[32,8,16,128]{3,2,1,0:T(8,128)}), f32[32,8,16,128]{3,2,1,0:T(8,128)}, u32[]{:S(2)}, u32[]{:S(2)}) %all-to-all-start.2) | async-done | bytes 2097184 | tf_op jit(solution)/shard_map/all_to_all | solution.py:287
  395.8 3.1 gram.5
  398.8 14.5 %all_to_all.25 = f32[8,160,128]{2,1,0:T(8,128)S(1)} all-to-all(f32[8,160,128]{2,1,0:T(8,128)S(1)} %bitcast.6), channel_id=1, replica_groups=mesh['ta'=4,'af'=8] {'af'}, dimensions={0} | all-to-all | bytes 1310720 | tf_op jit(solution)/shard_map/all_to_all | solution.py:224
  413.4 0.1 collective-permute-start
  413.5 2.4 collective-permute-start.1
  415.9 1.4 collective-permute-start.2
  417.3 3.4 collective-permute-done
  420.7 2.1 collective-permute-done.1
  422.9 13.5 %all_to_all.26 = f32[8,160,128]{2,1,0:T(8,128)S(1)} all-to-all(f32[8,160,128]{2,1,0:T(8,128)S(1)} %broadcast_in_dim.2), channel_id=1, replica_groups=mesh['ta'=4,'af'=8] {'af'}, dimensions={0} | all-to-all | bytes 1310720 | tf_op jit(solution)/shard_map/all_to_all | solution.py:234
  436.4 8.6 %iterate.1.subspace_ref = f32[64,512]{1,0:T(8,128)S(1)} custom-call(f32[1280,128]{1,0:T(8,128)S(1)} %bitcast.5, f32[64,512]{1,0:T(8,128)S(1)} %bitcast.7), custom_call_target="tpu_custom_call" | custom-call | tf_op jit(solution)/shard_map/iterate/pallas_call | solution.py:166
  445.0 10.9 %project.1 = f32[64,64,128]{2,1,0:T(8,128)} custom-call(f32[64,512]{1,0:T(8,128)S(1)} %iterate.1.subspace_ref, f32[32,8,16,128]{3,2,1,0:T(8,128)S(1)} %all-to-all-done.block_ref.refs_0_, f32[32,48,16,128]{3,2,1,0:T(8,128)} %all-to-all-done.1.block_ref.refs_1_, f32[32,8,16,128]{3,2,1,0:T(8,128)} %all-to-all-done.2.block_ref.refs_2_), custom_call_target="tpu_custom_call" | custom-call | tf_op jit(solution)/shard_map/project/pallas_call | solution.py:210
  (7 shorter events, 0.1 us)
Async XLA Ops:
  3.0 1.3 copy-start.1
  4.3 56.2 %all-to-all-start = ((f32[32,8,16,128]{3,2,1,0:T(8,128)}), f32[32,8,16,128]{3,2,1,0:T(8,128)S(1)}, u32[]{:S(2)}, u32[]{:S(2)}) async-start(f32[32,8,16,128]{3,2,1,0:T(8,128)} %copy-done.1), calls=%async_computation | async-start | bytes 4194304 | tf_op jit(solution)/shard_map/all_to_all | solution.py:287
  60.5 282.9 %all-to-all-start.1 = ((f32[32,48,16,128]{3,2,1,0:T(8,128)}), f32[32,48,16,128]{3,2,1,0:T(8,128)}, u32[]{:S(2)}, u32[]{:S(2)}) async-start(f32[32,48,16,128]{3,2,1,0:T(8,128)} %arrange.4), calls=%async_computation.1 | async-start | bytes 25165824 | tf_op jit(solution)/shard_map/all_to_all | solution.py:287
  67.7 1.3 copy-start
  343.4 52.4 %all-to-all-start.2 = ((f32[32,8,16,128]{3,2,1,0:T(8,128)}), f32[32,8,16,128]{3,2,1,0:T(8,128)}, u32[]{:S(2)}, u32[]{:S(2)}) async-start(f32[32,8,16,128]{3,2,1,0:T(8,128)} %copy-done), calls=%async_computation.2 | async-start | bytes 4194304 | tf_op jit(solution)/shard_map/all_to_all | solution.py:287
  398.8 37.6 %copy-start.2 = (f32[512,64]{0,1:T(8,128)S(1)}, f32[512,64]{0,1:T(8,128)}, u32[]{:S(2)}) copy-start(f32[512,64]{0,1:T(8,128)} %param.3) | copy-start | bytes 393220
  413.4 7.3 %collective-permute-start = (f32[160,128]{1,0:T(8,128)S(1)}, f32[160,128]{1,0:T(8,128)S(1)}, u32[]{:S(2)}, u32[]{:S(2)}) collective-permute-start(f32[160,128]{1,0:T(8,128)S(1)} %reduce_sum.9), channel_id=1, source_target_pairs={{0,8},{8,16},{16,24},{24,0},{1,9},{9,17},{17,25},{25,1},{2,10},{10... | collective-permute-start | bytes 245768 | tf_op jit(solution)/shard_map/ppermute | solution.py:230
  413.5 9.3 %collective-permute-start.1 = (f32[160,128]{1,0:T(8,128)S(1)}, f32[160,128]{1,0:T(8,128)S(1)}, u32[]{:S(2)}, u32[]{:S(2)}) collective-permute-start(f32[160,128]{1,0:T(8,128)S(1)} %reduce_sum.9), channel_id=1, source_target_pairs={{0,16},{8,24},{16,0},{24,8},{1,17},{9,25},{17,1},{25,9},{2,18},{10... | collective-permute-start | bytes 245768 | tf_op jit(solution)/shard_map/ppermute | solution.py:230
  415.9 6.9 %collective-permute-start.2 = (f32[160,128]{1,0:T(8,128)S(1)}, f32[160,128]{1,0:T(8,128)S(1)}, u32[]{:S(2)}, u32[]{:S(2)}) collective-permute-start(f32[160,128]{1,0:T(8,128)S(1)} %reduce_sum.9), channel_id=1, source_target_pairs={{0,24},{8,0},{16,8},{24,16},{1,25},{9,1},{17,9},{25,17},{2,26},{10... | collective-permute-start | bytes 245768 | tf_op jit(solution)/shard_map/ppermute | solution.py:230

commit v3 on v2

--- a/solution.py
+++ b/solution.py
@@ -1,5 +1,4 @@
 import functools
-import math
 
 import jax
 import jax.numpy as jnp
@@ -145,93 +144,142 @@
     return (work * scale)[:, size:]
 
 
-def iterate_kernel(packed_ref, basis_ref, out_ref, gram_ref):
-    group = packed_ref.shape[1]
+def iterate(matrix, subspace):
+    for _ in range(ITERS):
+        product = nn(subspace, matrix, HIGHEST)
+        inverse = inverse_cholesky(nt(product, product, HIGHEST))
+        subspace = nn(inverse, product, HIGHEST)
+    return subspace
+
+
+def unpack(place_ref, pieces, packed_ref, gram_ref):
+    rows, group = pieces[0].shape
+    for n, piece in enumerate(pieces):
+        packed_ref[pl.ds(pl.multiple_of(place_ref[n] * rows, 8), rows), :] = piece[...]
     for n, (i, j) in enumerate(lower_blocks(gram_ref.shape[0] // group)):
         block = packed_ref[n * group : (n + 1) * group, :]
         gram_ref[i * group : (i + 1) * group, j * group : (j + 1) * group] = block
         if i != j:
             gram_ref[j * group : (j + 1) * group, i * group : (i + 1) * group] = block.T
-    matrix = gram_ref[...]
-    subspace = basis_ref[...]
-    for _ in range(ITERS):
-        product = nn(subspace, matrix, HIGHEST)
-        inverse = inverse_cholesky(nt(product, product, HIGHEST))
-        subspace = nn(inverse, product, HIGHEST)
-    out_ref[...] = subspace
-
-
-def iterate(packed, basis_t):
-    planes_total = basis_t.shape[1]
+
+
+def finish_kernel(pieces_count, blocks_count, *refs):
+    place_ref, basis_ref = refs[:2]
+    pieces = refs[2 : 2 + pieces_count]
+    blocks = refs[2 + pieces_count : 2 + pieces_count + blocks_count]
+    rest = refs[2 + pieces_count + blocks_count :]
+    out_ref, packed_ref, gram_ref, result_ref, in_sems, out_sems = rest[:1] + rest[1:4] + rest[-2:]
+    held = rest[4:-2]
+    steps, first = [], 0
+    for n, block in enumerate(blocks):
+        for start in range(0, block.shape[1], PROJECT_CELLS):
+            size = min(PROJECT_CELLS, block.shape[1] - start)
+            cells = (slice(None), pl.ds(start, size))
+            copy = pltpu.make_async_copy(
+                block.at[cells], held[n].at[cells], in_sems.at[len(steps)]
+            )
+            copy.start()
+            steps.append((held[n].at[cells], pl.ds(first, size), copy))
+            first += size
+    unpack(place_ref, pieces, packed_ref, gram_ref)
+    subspace = iterate(gram_ref[...], basis_ref[...])
+    rank = subspace.shape[0]
+    basis_high, basis_low = split(subspace)
+    both = jnp.concatenate([basis_high, basis_low], axis=0)
+    copies = []
+    for n, (block, cells, arrival) in enumerate(steps):
+        arrival.wait()
+        cells_y = block.shape[3]
+        high, low = split(cell_matrix(block))
+        main = nn(both, high)
+        result = main[:rank] + (main[rank:] + nn(basis_high, low))
+        for i in range(cells.size):
+            result_ref[cells.start + i] = result[:, i * cells_y : (i + 1) * cells_y]
+        copy = pltpu.make_async_copy(result_ref.at[cells], out_ref.at[cells], out_sems.at[n])
+        copy.start()
+        copies.append(copy)
+    for copy in copies:
+        copy.wait()
+
+
+def finish(places, pieces, basis_t, blocks):
+    rank, planes_total = basis_t.shape
+    cells = sum(block.shape[1] for block in blocks)
+    cells_y = blocks[0].shape[3]
+    rows, group = pieces[0].shape
+    steps = sum(pl.cdiv(block.shape[1], PROJECT_CELLS) for block in blocks)
+    vmem = pl.BlockSpec(memory_space=pltpu.VMEM)
+    anywhere = pl.BlockSpec(memory_space=pl.ANY)
+    out_shape = (cells, rank, cells_y)
     return pl.pallas_call(
-        iterate_kernel,
-        out_shape=jax.ShapeDtypeStruct(basis_t.shape, jnp.float32),
-        scratch_shapes=[pltpu.VMEM((planes_total, planes_total), jnp.float32)],
+        functools.partial(finish_kernel, len(pieces), len(blocks)),
+        in_specs=[pl.BlockSpec(memory_space=pltpu.SMEM), vmem]
+        + [vmem] * len(pieces)
+        + [anywhere] * len(blocks),
+        out_specs=anywhere,
+        out_shape=jax.ShapeDtypeStruct(out_shape, jnp.float32),
+        scratch_shapes=[
+            pltpu.VMEM((rows * len(pieces), group), jnp.float32),
+            pltpu.VMEM((planes_total, planes_total), jnp.float32),
+            pltpu.VMEM(out_shape, jnp.float32),
+        ]
+        + [pltpu.VMEM(block.shape, jnp.float32) for block in blocks]
+        + [pltpu.SemaphoreType.DMA((steps,)), pltpu.SemaphoreType.DMA((steps,))],
         compiler_params=pltpu.CompilerParams(vmem_limit_bytes=VMEM_LIMIT),
-        name="iterate",
-    )(packed, basis_t)
-
-
-def project_kernel(steps, subspace_ref, *refs):
-    blocks, out_ref = refs[:-1], refs[-1]
-    rank = subspace_ref.shape[0]
-    basis_high, basis_low = split(subspace_ref[...])
-    both = jnp.concatenate([basis_high, basis_low], axis=0)
-    first = 0
-    for count, block_ref in zip(steps, blocks):
-
-        @pl.when((pl.program_id(0) >= first) & (pl.program_id(0) < first + count))
-        def _(block_ref=block_ref):
-            cells, cells_y = block_ref.shape[1], block_ref.shape[3]
-            high, low = split(cell_matrix(block_ref))
-            main = nn(both, high)
-            result = main[:rank] + (main[rank:] + nn(basis_high, low))
-            for i in range(cells):
-                out_ref[i] = result[:, i * cells_y : (i + 1) * cells_y]
-
-        first += count
-
-
-def project(subspace, blocks):
-    sources, _, planes, cells_y = blocks[0].shape
-    rank = subspace.shape[0]
-    cells = [block.shape[1] for block in blocks]
-    step = largest_step(math.gcd(*cells), PROJECT_CELLS)
-    steps = [count // step for count in cells]
-    in_specs = [pl.BlockSpec(subspace.shape, lambda i: (0, 0))]
-    for n, count in enumerate(steps):
-        first = sum(steps[:n])
-        in_specs.append(
-            pl.BlockSpec(
-                (sources, step, planes, cells_y),
-                lambda i, first=first, count=count: (0, jnp.clip(i - first, 0, count - 1), 0, 0),
-            )
-        )
-    return pl.pallas_call(
-        functools.partial(project_kernel, steps),
-        grid=(sum(steps),),
-        in_specs=in_specs,
-        out_specs=pl.BlockSpec((step, rank, cells_y), lambda i: (i, 0, 0)),
-        out_shape=jax.ShapeDtypeStruct((sum(cells), rank, cells_y), jnp.float32),
-        compiler_params=pltpu.CompilerParams(vmem_limit_bytes=VMEM_LIMIT),
-        name="project",
-    )(subspace, *blocks)
+        name="finish",
+    )(places, basis_t, *pieces, *blocks)
+
+
+def toward(i, step, count):
+    return i ^ step if count & (count - 1) == 0 else (i + step) % count
+
+
+def origin(i, step, count):
+    return i ^ step if count & (count - 1) == 0 else (i - step) % count
 
 
 def sum_over_devices(packed):
     groups_af, groups_ta = lax.axis_size("af"), lax.axis_size("ta")
-    rows = packed.shape[0] // groups_af
-    parts = lax.all_to_all(
-        packed.reshape(groups_af, rows, packed.shape[1]), "af", split_axis=0, concat_axis=0, tiled=True
-    )
-    mine = parts.sum(axis=0)
-    summed = mine
-    for distance in range(1, groups_ta):
-        summed = summed + lax.ppermute(
-            mine, "ta", [(i, (i + distance) % groups_ta) for i in range(groups_ta)]
+    inner = 2 if groups_af % 2 == 0 else 1
+    outer = groups_af // inner
+    me = lax.axis_index("af")
+    my_outer, my_inner = me // inner, me % inner
+
+    def to_inner(array):
+        return lax.ppermute(array, "af", [(i, i ^ 1) for i in range(groups_af)])
+
+    def to_outer(array, step):
+        return lax.ppermute(
+            array,
+            "af",
+            [(i, toward(i // inner, step, outer) * inner + i % inner) for i in range(groups_af)],
         )
-    spread = jnp.broadcast_to(summed[None], (groups_af,) + summed.shape)
-    return lax.all_to_all(spread, "af", split_axis=0, concat_axis=0, tiled=True).reshape(packed.shape)
+
+    def to_ta(array, step):
+        return lax.ppermute(array, "ta", [(i, toward(i, step, groups_ta)) for i in range(groups_ta)])
+
+    def pick(array, index):
+        return lax.dynamic_index_in_dim(array, index, 0, False)
+
+    def total(arrays):
+        return functools.reduce(jnp.add, arrays)
+
+    parts = packed.reshape(inner, -1, packed.shape[1])
+    mine = pick(parts, my_inner)
+    if inner == 2:
+        mine = mine + to_inner(pick(parts, 1 - my_inner))
+    parts = mine.reshape(outer, -1, packed.shape[1])
+    mine = total(
+        [pick(parts, my_outer)]
+        + [to_outer(pick(parts, toward(my_outer, k, outer)), k) for k in range(1, outer)]
+    )
+    mine = total([mine] + [to_ta(mine, k) for k in range(1, groups_ta)])
+    pieces = [mine] + [to_outer(mine, k) for k in range(1, outer)]
+    places = [my_inner * outer + origin(my_outer, k, outer) for k in range(outer)]
+    if inner == 2:
+        pieces += [to_inner(piece) for piece in pieces]
+        places += [(1 - my_inner) * outer + origin(my_outer, k, outer) for k in range(outer)]
+    return pieces, jnp.stack(places).astype(jnp.int32)
 
 
 def arrange_kernel(in_ref, out_ref):
@@ -292,9 +340,8 @@
         ]
     total = gram(blocks[0], None)
     total = gram(blocks[1], total)
-    packed = sum_over_devices(gram(blocks[2], total, groups_af))
-    subspace = iterate(packed, initial_basis.T)
-    core = project(subspace, blocks)
+    pieces, places = sum_over_devices(gram(blocks[2], total, groups_af))
+    core = finish(places, pieces, initial_basis.T, blocks)
     return core.reshape(block_frames, block_x, core.shape[1], cells_y)
 
 

time: 457 us -> 444 us (0.972)
  blocking collectives: 28.1 us -> 0 us
  waiting for transfers between devices: 343 us -> 352 us
  starting transfers between devices: 18.8 us -> 26.5 us
    all_to_all x2 -> x0, blocking collectives: 28.1 us -> none  [the longest x1 14.5 us: sum_over_devices(): lax.all_to_all(packed.reshape(groups_af, rows, packed.shape[1]), 'af', sp...]
    ppermute x3 -> x14, waiting for transfers between devices: 5.48 us -> 14.6 us  [the longest x6 7.46 us: to_outer(): lax.ppermute(array, 'af', [(i, toward(i // inner, step, outer) * inner +...]
    ppermute x3 -> x14, starting transfers between devices: 3.87 us -> 11.6 us  [the longest x6 7.11 us: to_outer(): lax.ppermute(array, 'af', [(i, toward(i // inner, step, outer) * inner +...]
    pallas_call x2 -> x1, Pallas kernels: 19.5 us -> 15.9 us  [finish(): pl.pallas_call(functools.partial(finish_kernel, len(pieces), len(blocks))...]
  transfers between devices with their start and end apart: 6 -> 17, of which waited for: 5 -> 14; matrix products, arithmetic and copies ran while one was open for 0% -> 0% of each run, Pallas kernels for 8% -> 9%
where the time goes in v3:
time: 444 us; the launch traced here: 443 us
  waiting for transfers between devices  352 us (79%)
  Pallas kernels  59.9 us (13%)
  starting transfers between devices  26.5 us (6%)
    all_to_all x3, waiting for transfers between devices, local(): lax.all_to_all(block, ('ta', 'af'), split_axis=0, concat_axis=0, tiled=True)  337 us
    pallas_call x3, Pallas kernels, outgoing(): pl.pallas_call(arrange_kernel, grid=(groups_ta, count // part), in_specs=...  26.1 us
    pallas_call x3, Pallas kernels, gram(): pl.pallas_call(kernel, grid=(cells // step,), in_specs=in_specs, out_spec...  18 us
    pallas_call x1, Pallas kernels, finish(): pl.pallas_call(functools.partial(finish_kernel, len(pieces), len(blocks))...  15.9 us
    all_to_all x3, starting transfers between devices, local(): lax.all_to_all(block, ('ta', 'af'), split_axis=0, concat_axis=0, tiled=True)  14.9 us
  transfers between devices with their start and end apart: 17, of which 14 were waited for; matrix products, arithmetic and copies ran while one was open for 0% of the time, Pallas kernels for 9%

profile of v3, /device:TPU:0, one launch (start us, length us, event | category | flops | bytes accessed | tf_op | source)
XLA Modules:
  0.0 443.3 jit_solution(3645087517344670147)
XLA Ops:
  0.0 3.0 arrange.5
  4.3 7.3 %all-to-all-start = ((f32[32,8,16,128]{3,2,1,0:T(8,128)}), f32[32,8,16,128]{3,2,1,0:T(8,128)S(1)}, u32[]{:S(2)}, u32[]{:S(2)}) async-start(f32[32,8,16,128]{3,2,1,0:T(8,128)} %copy-done.1), calls=%async_computation | async-start | bytes 4194304 | tf_op jit(solution)/shard_map/all_to_all | solution.py:335
  11.6 20.1 %arrange.4 = f32[32,48,16,128]{3,2,1,0:T(8,128)} custom-call(f32[16,16,8,16,128]{4,3,2,1,0:T(8,128)} %bitcast.33), custom_call_target="tpu_custom_call" | custom-call | tf_op jit(solution)/shard_map/arrange/pallas_call | solution.py:307
  31.7 28.8 %all-to-all-done.block_ref.refs_10_ = f32[32,8,16,128]{3,2,1,0:T(8,128)S(1)} async-done(((f32[32,8,16,128]{3,2,1,0:T(8,128)}), f32[32,8,16,128]{3,2,1,0:T(8,128)S(1)}, u32[]{:S(2)}, u32[]{:S(2)}) %all-to-all-start) | async-done | bytes 2097184 | tf_op jit(solution)/shard_map/all_to_all | solution.py:335
  60.5 4.1 all-to-all-start.1
  64.6 3.0 arrange.3
  69.0 274.4 %all-to-all-done.1.block_ref.refs_11_ = f32[32,48,16,128]{3,2,1,0:T(8,128)} async-done(((f32[32,48,16,128]{3,2,1,0:T(8,128)}), f32[32,48,16,128]{3,2,1,0:T(8,128)}, u32[]{:S(2)}, u32[]{:S(2)}) %all-to-all-start.1) | async-done | bytes 12582944 | tf_op jit(solution)/shard_map/all_to_all | solution.py:335
  343.4 3.5 all-to-all-start.2
  346.9 1.7 gram.3.before_ref
  348.6 13.2 %gram.4.before_ref = f32[512,512]{1,0:T(8,128)S(1)} custom-call(f32[32,48,16,128]{3,2,1,0:T(8,128)} %all-to-all-done.1.block_ref.refs_11_, f32[512,512]{1,0:T(8,128)S(1)} %gram.3.before_ref), custom_call_target="tpu_custom_call" | custom-call | tf_op jit(solution)/shard_map/gram/pallas_call | solution.py:113
  361.8 34.0 %all-to-all-done.2.block_ref.refs_12_ = f32[32,8,16,128]{3,2,1,0:T(8,128)} async-done(((f32[32,8,16,128]{3,2,1,0:T(8,128)}), f32[32,8,16,128]{3,2,1,0:T(8,128)}, u32[]{:S(2)}, u32[]{:S(2)}) %all-to-all-start.2) | async-done | bytes 2097184 | tf_op jit(solution)/shard_map/all_to_all | solution.py:335
  395.8 3.1 gram.5
  399.8 1.6 collective-permute-done
  402.4 1.4 collective-permute-start.1
  403.8 1.5 collective-permute-start.2
  407.0 2.0 collective-permute-done.2
  409.0 1.6 collective-permute-done.3
  410.7 2.4 collective-permute-start.5
  413.1 1.9 collective-permute-start.6
  415.1 2.8 collective-permute-done.5
  418.0 1.5 collective-permute-done.6
  420.6 2.5 collective-permute-start.9
  424.5 1.4 collective-permute-done.9.refs_5_
  427.2 15.9 %finish.1 = f32[64,64,128]{2,1,0:T(8,128)} custom-call(s32[8]{0:T(128)S(1)} %stack.35.refs_0_, f32[64,512]{1,0:T(8,128)S(1)} %bitcast.31, f32[160,128]{1,0:T(8,128)S(1)} %add_add_fusion.refs_2_, f32[160,128]{1,0:T(8,128)S(1)} %collective-permute-done.7.refs_3_, f32[160,128]{1,0:T(8,128)S(1)} %collective-permute-done.8.refs_4_, ...), custom_call_target="tpu_custom_call" | custom-call | tf_op jit(solution)/shard_map/finish/pallas_call | solution.py:214
  (31 shorter events, 10.3 us)
Async XLA Ops:
  3.0 1.3 copy-start.1
  4.3 56.2 %all-to-all-start = ((f32[32,8,16,128]{3,2,1,0:T(8,128)}), f32[32,8,16,128]{3,2,1,0:T(8,128)S(1)}, u32[]{:S(2)}, u32[]{:S(2)}) async-start(f32[32,8,16,128]{3,2,1,0:T(8,128)} %copy-done.1), calls=%async_computation | async-start | bytes 4194304 | tf_op jit(solution)/shard_map/all_to_all | solution.py:335
  60.5 282.9 %all-to-all-start.1 = ((f32[32,48,16,128]{3,2,1,0:T(8,128)}), f32[32,48,16,128]{3,2,1,0:T(8,128)}, u32[]{:S(2)}, u32[]{:S(2)}) async-start(f32[32,48,16,128]{3,2,1,0:T(8,128)} %arrange.4), calls=%async_computation.1 | async-start | bytes 25165824 | tf_op jit(solution)/shard_map/all_to_all | solution.py:335
  67.7 1.3 copy-start
  343.4 52.4 %all-to-all-start.2 = ((f32[32,8,16,128]{3,2,1,0:T(8,128)}), f32[32,8,16,128]{3,2,1,0:T(8,128)}, u32[]{:S(2)}, u32[]{:S(2)}) async-start(f32[32,8,16,128]{3,2,1,0:T(8,128)} %copy-done), calls=%async_computation.2 | async-start | bytes 4194304 | tf_op jit(solution)/shard_map/all_to_all | solution.py:335
  398.8 0.8 copy-start.2
  398.9 28.4 %copy-start.3 = (f32[512,64]{0,1:T(8,128)S(1)}, f32[512,64]{0,1:T(8,128)}, u32[]{:S(2)}) copy-start(f32[512,64]{0,1:T(8,128)} %param.3) | copy-start | bytes 393220
  399.7 1.7 collective-permute-start
  402.4 4.6 %collective-permute-start.1 = (f32[160,128]{1,0:T(8,128)S(1)}, f32[160,128]{1,0:T(8,128)S(1)}, u32[]{:S(2)}, u32[]{:S(2)}) collective-permute-start(f32[160,128]{1,0:T(8,128)S(1)} %get-tuple-element.13), channel_id=1, source_target_pairs={{0,2},{1,3},{2,0},{3,1},{4,6},{5,7},{6,4},{7,5},{8,10},{9,11},{10,... | collective-permute-start | bytes 245768 | tf_op jit(solution)/shard_map/ppermute | solution.py:252
  403.8 5.2 %collective-permute-start.2 = (f32[160,128]{1,0:T(8,128)S(1)}, f32[160,128]{1,0:T(8,128)S(1)}, u32[]{:S(2)}, u32[]{:S(2)}) collective-permute-start(f32[160,128]{1,0:T(8,128)S(1)} %get-tuple-element.15), channel_id=1, source_target_pairs={{0,4},{1,5},{2,6},{3,7},{4,0},{5,1},{6,2},{7,3},{8,12},{9,13},{10,... | collective-permute-start | bytes 245768 | tf_op jit(solution)/shard_map/ppermute | solution.py:252
  405.3 5.3 %collective-permute-start.3 = (f32[160,128]{1,0:T(8,128)S(1)}, f32[160,128]{1,0:T(8,128)S(1)}, u32[]{:S(2)}, u32[]{:S(2)}) collective-permute-start(f32[160,128]{1,0:T(8,128)S(1)} %get-tuple-element.14), channel_id=1, source_target_pairs={{0,6},{1,7},{2,4},{3,5},{4,2},{5,3},{6,0},{7,1},{8,14},{9,15},{10,... | collective-permute-start | bytes 245768 | tf_op jit(solution)/shard_map/ppermute | solution.py:252
  410.6 4.5 %collective-permute-start.4 = (f32[160,128]{1,0:T(8,128)S(1)}, f32[160,128]{1,0:T(8,128)S(1)}, u32[]{:S(2)}, u32[]{:S(2)}) collective-permute-start(f32[160,128]{1,0:T(8,128)S(1)} %fusion.1), channel_id=1, source_target_pairs={{0,8},{8,0},{16,24},{24,16},{1,9},{9,1},{17,25},{25,17},{2,10},{10... | collective-permute-start | bytes 245768 | tf_op jit(solution)/shard_map/ppermute | solution.py:259
  410.7 7.3 %collective-permute-start.5 = (f32[160,128]{1,0:T(8,128)S(1)}, f32[160,128]{1,0:T(8,128)S(1)}, u32[]{:S(2)}, u32[]{:S(2)}) collective-permute-start(f32[160,128]{1,0:T(8,128)S(1)} %fusion.1), channel_id=1, source_target_pairs={{0,16},{8,24},{16,0},{24,8},{1,17},{9,25},{17,1},{25,9},{2,18},{10... | collective-permute-start | bytes 245768 | tf_op jit(solution)/shard_map/ppermute | solution.py:259
  413.1 6.3 %collective-permute-start.6 = (f32[160,128]{1,0:T(8,128)S(1)}, f32[160,128]{1,0:T(8,128)S(1)}, u32[]{:S(2)}, u32[]{:S(2)}) collective-permute-start(f32[160,128]{1,0:T(8,128)S(1)} %fusion.1), channel_id=1, source_target_pairs={{0,24},{8,16},{16,8},{24,0},{1,25},{9,17},{17,9},{25,1},{2,26},{10... | collective-permute-start | bytes 245768 | tf_op jit(solution)/shard_map/ppermute | solution.py:259
  419.5 4.5 %collective-permute-start.7 = (f32[160,128]{1,0:T(8,128)S(1)}, f32[160,128]{1,0:T(8,128)S(1)}, u32[]{:S(2)}, u32[]{:S(2)}) collective-permute-start(f32[160,128]{1,0:T(8,128)S(1)} %add_add_fusion.refs_2_), channel_id=1, source_target_pairs={{0,2},{1,3},{2,0},{3,1},{4,6},{5,7},{6,4},{7,5},{8,10},{9,11},{10,... | collective-permute-start | bytes 245768 | tf_op jit(solution)/shard_map/ppermute | solution.py:252
  420.1 4.4 %collective-permute-start.8 = (f32[160,128]{1,0:T(8,128)S(1)}, f32[160,128]{1,0:T(8,128)S(1)}, u32[]{:S(2)}, u32[]{:S(2)}) collective-permute-start(f32[160,128]{1,0:T(8,128)S(1)} %add_add_fusion.refs_2_), channel_id=1, source_target_pairs={{0,4},{1,5},{2,6},{3,7},{4,0},{5,1},{6,2},{7,3},{8,12},{9,13},{10,... | collective-permute-start | bytes 245768 | tf_op jit(solution)/shard_map/ppermute | solution.py:252
  420.6 5.3 %collective-permute-start.9 = (f32[160,128]{1,0:T(8,128)S(1)}, f32[160,128]{1,0:T(8,128)S(1)}, u32[]{:S(2)}, u32[]{:S(2)}) collective-permute-start(f32[160,128]{1,0:T(8,128)S(1)} %add_add_fusion.refs_2_), channel_id=1, source_target_pairs={{0,6},{1,7},{2,4},{3,5},{4,2},{5,3},{6,0},{7,1},{8,14},{9,15},{10,... | collective-permute-start | bytes 245768 | tf_op jit(solution)/shard_map/ppermute | solution.py:252
  423.1 3.0 collective-permute-start.10
  424.0 2.0 collective-permute-start.11
  424.5 1.5 collective-permute-start.12
  425.9 1.3 collective-permute-start.13

commit v4 on v3

--- a/solution.py
+++ b/solution.py
@@ -9,9 +9,10 @@
 
 ITERS = 3
 HIGHEST = lax.Precision.HIGHEST
-VMEM_LIMIT = 48 * 1024 * 1024
-PIVOTS = 8
-GRAM_CELLS = 4
+MIB = 1024 * 1024
+PIVOTS = 16
+GRAM_CELLS = 8
+PACK_CELLS = 4
 PROJECT_CELLS = 8
 
 
@@ -71,55 +72,103 @@
 
     add_products(block_ref, total_ref)
 
+    @pl.when(pl.program_id(0) == pl.num_programs(0) - 1)
+    def _():
+        total = total_ref[...]
+        total_ref[...] = 0.5 * (total + total.T)
+
 
 def lower_blocks(count):
     return [(i, j) for i in range(count) for j in range(i + 1)]
 
 
-def gram_pack_kernel(block_ref, before_ref, packed_ref, total_ref):
-    gram_more_kernel(block_ref, before_ref, total_ref)
-
-    @pl.when(pl.program_id(0) == pl.num_programs(0) - 1)
+def gram_pack_kernel(place_ref, block_ref, before_ref, *refs):
+    parts, total_ref = refs[:-1], refs[-1]
+    rows, group = parts[0].shape
+    planes_total = before_ref.shape[0]
+    half = planes_total // 2 // group * group
+
+    def add(before):
+        high, low = split(cell_matrix(block_ref))
+        left = jnp.concatenate([high, high, low], axis=1)
+        right = jnp.concatenate([high, low, high], axis=1)
+        total_ref[:half, :half] = before[:half, :half] + nt(left[:half], right[:half])
+        total_ref[half:, :] = before[half:, :] + nt(left[half:], right)
+
+    @pl.when(pl.program_id(0) == 0)
     def _():
-        group = packed_ref.shape[1]
-        blocks = lower_blocks(total_ref.shape[0] // group)
-        for n, (i, j) in enumerate(blocks):
-            block = total_ref[i * group : (i + 1) * group, j * group : (j + 1) * group]
-            mirrored = total_ref[j * group : (j + 1) * group, i * group : (i + 1) * group]
-            packed_ref[n * group : (n + 1) * group, :] = 0.5 * (block + mirrored.T)
-        rest = packed_ref.shape[0] - len(blocks) * group
-        if rest:
-            packed_ref[len(blocks) * group :, :] = jnp.zeros((rest, group), jnp.float32)
-
-
-def gram(block, before, parts=None):
+        add(before_ref)
+
+    @pl.when(pl.program_id(0) > 0)
+    def _():
+        add(total_ref)
+
+    blocks = lower_blocks(planes_total // group)
+    for place in range(len(parts)):
+
+        @pl.when((pl.program_id(0) == pl.num_programs(0) - 1) & (place_ref[0] == place))
+        def _(place=place):
+            for k, part_ref in enumerate(parts):
+                start = (place + k) % len(parts) * rows
+                copy_rows(part_ref, start, blocks, total_ref, group)
+
+
+def copy_rows(part_ref, start, blocks, total_ref, group):
+    done = 0
+    while done < part_ref.shape[0]:
+        n, skip = divmod(start + done, group)
+        size = min(group - skip, part_ref.shape[0] - done)
+        if n < len(blocks):
+            i, j = blocks[n]
+            value = total_ref[
+                i * group + skip : i * group + skip + size, j * group : (j + 1) * group
+            ]
+        else:
+            value = jnp.zeros((size, group), jnp.float32)
+        part_ref[done : done + size, :] = value
+        done += size
+
+
+def gram(block, before):
     sources, cells, planes, cells_y = block.shape
     planes_total = sources * planes
     step = largest_step(cells, GRAM_CELLS)
     square = (planes_total, planes_total)
     whole = pl.BlockSpec(square, lambda i: (0, 0))
     in_specs = [pl.BlockSpec((sources, step, planes, cells_y), lambda i: (0, i, 0, 0))]
-    operands = [block]
-    kernel, out_shape, scratch = gram_kernel, square, []
-    if before is not None:
-        in_specs.append(whole)
-        operands.append(before)
-        kernel = gram_more_kernel
-    if parts is not None:
-        group = planes_total // largest_step(planes_total, planes_total // 128)
-        rows = len(lower_blocks(planes_total // group)) * group
-        out_shape = (rows + -rows % (8 * parts), group)
-        kernel, scratch = gram_pack_kernel, [pltpu.VMEM(square, jnp.float32)]
     return pl.pallas_call(
-        kernel,
+        gram_kernel if before is None else gram_more_kernel,
         grid=(cells // step,),
-        in_specs=in_specs,
-        out_specs=pl.BlockSpec(out_shape, lambda i: (0, 0)),
-        out_shape=jax.ShapeDtypeStruct(out_shape, jnp.float32),
-        scratch_shapes=scratch,
-        compiler_params=pltpu.CompilerParams(vmem_limit_bytes=VMEM_LIMIT),
+        in_specs=in_specs if before is None else in_specs + [whole],
+        out_specs=whole,
+        out_shape=jax.ShapeDtypeStruct(square, jnp.float32),
+        compiler_params=pltpu.CompilerParams(vmem_limit_bytes=20 * MIB),
         name="gram",
-    )(*operands)
+    )(*([block] if before is None else [block, before]))
+
+
+def gram_pack(block, before, place, parts, devices):
+    planes_total = before.shape[0]
+    group = planes_total // largest_step(planes_total, planes_total // 128)
+    rows = len(lower_blocks(planes_total // group)) * group
+    rows += -rows % (8 * devices)
+    sources, cells, planes, cells_y = block.shape
+    step = largest_step(cells, PACK_CELLS)
+    vmem = pl.BlockSpec(memory_space=pltpu.VMEM)
+    return pl.pallas_call(
+        gram_pack_kernel,
+        grid=(cells // step,),
+        in_specs=[
+            pl.BlockSpec(memory_space=pltpu.SMEM),
+            pl.BlockSpec((sources, step, planes, cells_y), lambda i: (0, i, 0, 0)),
+            vmem,
+        ],
+        out_specs=[vmem] * parts,
+        out_shape=[jax.ShapeDtypeStruct((rows // parts, group), jnp.float32)] * parts,
+        scratch_shapes=[pltpu.VMEM(before.shape, jnp.float32)],
+        compiler_params=pltpu.CompilerParams(vmem_limit_bytes=20 * MIB),
+        name="gram_pack",
+    )(place.astype(jnp.int32).reshape(1), block, before)
 
 
 def inverse_cholesky(matrix):
@@ -225,7 +274,7 @@
         ]
         + [pltpu.VMEM(block.shape, jnp.float32) for block in blocks]
         + [pltpu.SemaphoreType.DMA((steps,)), pltpu.SemaphoreType.DMA((steps,))],
-        compiler_params=pltpu.CompilerParams(vmem_limit_bytes=VMEM_LIMIT),
+        compiler_params=pltpu.CompilerParams(vmem_limit_bytes=32 * MIB),
         name="finish",
     )(places, basis_t, *pieces, *blocks)
 
@@ -238,9 +287,13 @@
     return i ^ step if count & (count - 1) == 0 else (i - step) % count
 
 
-def sum_over_devices(packed):
+def inner_size():
+    return 2 if lax.axis_size("af") % 2 == 0 else 1
+
+
+def sum_over_devices(parts):
     groups_af, groups_ta = lax.axis_size("af"), lax.axis_size("ta")
-    inner = 2 if groups_af % 2 == 0 else 1
+    inner = inner_size()
     outer = groups_af // inner
     me = lax.axis_index("af")
     my_outer, my_inner = me // inner, me % inner
@@ -264,11 +317,10 @@
     def total(arrays):
         return functools.reduce(jnp.add, arrays)
 
-    parts = packed.reshape(inner, -1, packed.shape[1])
-    mine = pick(parts, my_inner)
+    mine = parts[0]
     if inner == 2:
-        mine = mine + to_inner(pick(parts, 1 - my_inner))
-    parts = mine.reshape(outer, -1, packed.shape[1])
+        mine = mine + to_inner(parts[1])
+    parts = mine.reshape(outer, -1, mine.shape[1])
     mine = total(
         [pick(parts, my_outer)]
         + [to_outer(pick(parts, toward(my_outer, k, outer)), k) for k in range(1, outer)]
@@ -282,10 +334,28 @@
     return pieces, jnp.stack(places).astype(jnp.int32)
 
 
-def arrange_kernel(in_ref, out_ref):
-    for x in range(in_ref.shape[3]):
-        for target in range(in_ref.shape[2]):
-            out_ref[target, x] = in_ref[0, :, target, x]
+def arrange_kernel(spots, in_ref, out_ref, held_ref, ready_ref, in_sems, out_sems):
+    part, targets = held_ref.shape[3], held_ref.shape[2]
+    arrivals, sent = [], []
+    for n, (frame, x, _, _) in enumerate(spots):
+        copy = pltpu.make_async_copy(
+            in_ref.at[frame, :, :, pl.ds(x, part)], held_ref.at[n], in_sems.at[n]
+        )
+        copy.start()
+        arrivals.append(copy)
+    for n, (_, _, group, cell) in enumerate(spots):
+        arrivals[n].wait()
+        for target in range(targets):
+            ready_ref[n, target] = jnp.swapaxes(held_ref[n, :, target], 0, 1)
+        copy = pltpu.make_async_copy(
+            ready_ref.at[n],
+            out_ref.at[pl.ds(group * targets, targets), pl.ds(cell, part)],
+            out_sems.at[n],
+        )
+        copy.start()
+        sent.append(copy)
+    for copy in sent:
+        copy.wait()
 
 
 def outgoing(velocity, first, count):
@@ -298,21 +368,24 @@
         ordered = ordered.transpose(0, 3, 1, 4, 2, 5)
         ordered = ordered.reshape(groups_ta * groups_af, -1, planes, cells_y)
         return ordered[:, first : first + count]
-    parts_x, start = block_x // part, first // part
-
-    def source(group, i):
-        frame = group * block_frames + (start + i) // parts_x
-        return frame, 0, 0, lax.rem(start + i, parts_x), 0
-
+    spots = [
+        (group * block_frames + cell // block_x, cell % block_x, group, cell - first)
+        for group in range(groups_ta)
+        for cell in range(first, first + count, part)
+    ]
+    anywhere = pl.BlockSpec(memory_space=pl.ANY)
     return pl.pallas_call(
-        arrange_kernel,
-        grid=(groups_ta, count // part),
-        in_specs=[pl.BlockSpec((1, planes, groups_af, part, cells_y), source)],
-        out_specs=pl.BlockSpec((groups_af, part, planes, cells_y), lambda group, i: (group, i, 0, 0)),
-        out_shape=jax.ShapeDtypeStruct(
-            (groups_ta * groups_af, count, planes, cells_y), jnp.float32
-        ),
-        compiler_params=pltpu.CompilerParams(vmem_limit_bytes=VMEM_LIMIT),
+        functools.partial(arrange_kernel, spots),
+        in_specs=[anywhere],
+        out_specs=anywhere,
+        out_shape=pltpu.HBM((groups_ta * groups_af, count, planes, cells_y), jnp.float32),
+        scratch_shapes=[
+            pltpu.VMEM((len(spots), planes, groups_af, part, cells_y), jnp.float32),
+            pltpu.VMEM((len(spots), groups_af, part, planes, cells_y), jnp.float32),
+            pltpu.SemaphoreType.DMA((len(spots),)),
+            pltpu.SemaphoreType.DMA((len(spots),)),
+        ],
+        compiler_params=pltpu.CompilerParams(vmem_limit_bytes=56 * MIB),
         name="arrange",
     )(velocity.reshape(frames, planes, groups_af, block_x, cells_y))
 
@@ -340,7 +413,9 @@
         ]
     total = gram(blocks[0], None)
     total = gram(blocks[1], total)
-    pieces, places = sum_over_devices(gram(blocks[2], total, groups_af))
+    inner = inner_size()
+    parts = gram_pack(blocks[2], total, lax.axis_index("af") % inner, inner, groups_af)
+    pieces, places = sum_over_devices(parts)
     core = finish(places, pieces, initial_basis.T, blocks)
     return core.reshape(block_frames, block_x, core.shape[1], cells_y)
 

time: 444 us -> 440 us (level)
  waiting for transfers between devices: 352 us -> 368 us
  Pallas kernels: 59.9 us -> 45.3 us
    all_to_all x3, waiting for transfers between devices: 337 us -> 353 us  [local(): lax.all_to_all(block, ('ta', 'af'), split_axis=0, concat_axis=0, tiled=True)]
    pallas_call x6, Pallas kernels: 44 us -> 29.9 us  [the longest x3 14.4 us: outgoing(): pl.pallas_call(functools.partial(arrange_kernel, spots), in_specs=[anywhe...]
  transfers between devices with their start and end apart: 17 -> 17, of which waited for: 14 -> 14; matrix products, arithmetic and copies ran while one was open for 0% -> 0% of each run, Pallas kernels for 9% -> 5%
where the time goes in v4:
time: 440 us
  waiting for transfers between devices  368 us (84%)
  Pallas kernels  45.3 us (10%)
  starting transfers between devices  26.5 us (6%)
    all_to_all x3, waiting for transfers between devices, local(): lax.all_to_all(block, ('ta', 'af'), split_axis=0, concat_axis=0, tiled=True)  353 us
    pallas_call x1, Pallas kernels, finish(): pl.pallas_call(functools.partial(finish_kernel, len(pieces), len(blocks))...  15.4 us
    all_to_all x3, starting transfers between devices, local(): lax.all_to_all(block, ('ta', 'af'), split_axis=0, concat_axis=0, tiled=True)  14.9 us
    pallas_call x3, Pallas kernels, outgoing(): pl.pallas_call(functools.partial(arrange_kernel, spots), in_specs=[anywhe...  14.4 us
    pallas_call x2, Pallas kernels, gram(): pl.pallas_call(gram_kernel if before is None else gram_more_kernel, grid=...  11.8 us
  transfers between devices with their start and end apart: 17, of which 14 were waited for; matrix products, arithmetic and copies ran while one was open for 0% of the time, Pallas kernels for 5%

profile of v4, /device:TPU:0, one launch (start us, length us, event | category | flops | bytes accessed | tf_op | source)
XLA Modules:
  0.0 439.9 jit_solution(15493734659194674481)
XLA Ops:
  0.0 2.5 arrange.5
  2.5 7.3 %all-to-all-start = ((f32[32,8,16,128]{3,2,1,0:T(8,128)}), f32[32,8,16,128]{3,2,1,0:T(8,128)S(1)}, u32[]{:S(2)}, u32[]{:S(2)}) async-start(f32[32,8,16,128]{3,2,1,0:T(8,128)} %arrange.5), calls=%async_computation | async-start | bytes 4194304 | tf_op jit(solution)/shard_map/all_to_all | solution.py:408
  9.8 9.4 %arrange.4 = f32[32,48,16,128]{3,2,1,0:T(8,128)} custom-call(f32[16,16,8,16,128]{4,3,2,1,0:T(8,128)} %bitcast.27), custom_call_target="tpu_custom_call" | custom-call | tf_op jit(solution)/shard_map/arrange/pallas_call | solution.py:377
  19.2 39.5 %all-to-all-done.block_ref.refs_10_ = f32[32,8,16,128]{3,2,1,0:T(8,128)S(1)} async-done(((f32[32,8,16,128]{3,2,1,0:T(8,128)}), f32[32,8,16,128]{3,2,1,0:T(8,128)S(1)}, u32[]{:S(2)}, u32[]{:S(2)}) %all-to-all-start) | async-done | bytes 2097184 | tf_op jit(solution)/shard_map/all_to_all | solution.py:408
  58.7 4.1 all-to-all-start.1
  62.9 2.5 arrange.3
  65.4 276.2 %all-to-all-done.1.block_ref.refs_11_ = f32[32,48,16,128]{3,2,1,0:T(8,128)} async-done(((f32[32,48,16,128]{3,2,1,0:T(8,128)}), f32[32,48,16,128]{3,2,1,0:T(8,128)}, u32[]{:S(2)}, u32[]{:S(2)}) %all-to-all-start.1) | async-done | bytes 12582944 | tf_op jit(solution)/shard_map/all_to_all | solution.py:408
  341.6 3.5 all-to-all-start.2
  345.1 1.3 gram.2.before_ref
  346.4 10.5 %gram.3.before_ref = f32[512,512]{1,0:T(8,128)S(1)} custom-call(f32[32,48,16,128]{3,2,1,0:T(8,128)} %all-to-all-done.1.block_ref.refs_11_, f32[512,512]{1,0:T(8,128)S(1)} %gram.2.before_ref), custom_call_target="tpu_custom_call" | custom-call | tf_op jit(solution)/shard_map/gram/pallas_call | solution.py:139
  356.9 37.1 %all-to-all-done.2.block_ref.refs_12_ = f32[32,8,16,128]{3,2,1,0:T(8,128)} async-done(((f32[32,8,16,128]{3,2,1,0:T(8,128)}), f32[32,8,16,128]{3,2,1,0:T(8,128)}, u32[]{:S(2)}, u32[]{:S(2)}) %all-to-all-start.2) | async-done | bytes 2097184 | tf_op jit(solution)/shard_map/all_to_all | solution.py:408
  394.0 3.7 gram_pack.1
  397.7 1.8 collective-permute-done
  399.6 1.4 collective-permute-start.1
  401.0 1.5 collective-permute-start.2
  404.2 2.0 collective-permute-done.2
  406.2 1.6 collective-permute-done.3
  407.9 2.4 collective-permute-start.5
  410.3 1.9 collective-permute-start.6
  412.3 2.8 collective-permute-done.5
  415.1 1.5 collective-permute-done.6
  417.7 2.5 collective-permute-start.9
  421.7 1.4 collective-permute-done.9.refs_5_
  424.4 15.4 %finish.1 = f32[64,64,128]{2,1,0:T(8,128)} custom-call(s32[8]{0:T(128)S(1)} %stack.35.refs_0_, f32[64,512]{1,0:T(8,128)S(1)} %bitcast.25, f32[160,128]{1,0:T(8,128)S(1)} %add_add_fusion.refs_2_, f32[160,128]{1,0:T(8,128)S(1)} %collective-permute-done.7.refs_3_, f32[160,128]{1,0:T(8,128)S(1)} %collective-permute-done.8.refs_4_, ...), custom_call_target="tpu_custom_call" | custom-call | tf_op jit(solution)/shard_map/finish/pallas_call | solution.py:263
  (24 shorter events, 5.8 us)
Async XLA Ops:
  2.5 56.2 %all-to-all-start = ((f32[32,8,16,128]{3,2,1,0:T(8,128)}), f32[32,8,16,128]{3,2,1,0:T(8,128)S(1)}, u32[]{:S(2)}, u32[]{:S(2)}) async-start(f32[32,8,16,128]{3,2,1,0:T(8,128)} %arrange.5), calls=%async_computation | async-start | bytes 4194304 | tf_op jit(solution)/shard_map/all_to_all | solution.py:408
  58.7 282.9 %all-to-all-start.1 = ((f32[32,48,16,128]{3,2,1,0:T(8,128)}), f32[32,48,16,128]{3,2,1,0:T(8,128)}, u32[]{:S(2)}, u32[]{:S(2)}) async-start(f32[32,48,16,128]{3,2,1,0:T(8,128)} %arrange.4), calls=%async_computation.1 | async-start | bytes 25165824 | tf_op jit(solution)/shard_map/all_to_all | solution.py:408
  341.6 52.4 %all-to-all-start.2 = ((f32[32,8,16,128]{3,2,1,0:T(8,128)}), f32[32,8,16,128]{3,2,1,0:T(8,128)}, u32[]{:S(2)}, u32[]{:S(2)}) async-start(f32[32,8,16,128]{3,2,1,0:T(8,128)} %arrange.3), calls=%async_computation.2 | async-start | bytes 4194304 | tf_op jit(solution)/shard_map/all_to_all | solution.py:408
  397.7 26.7 %copy-start = (f32[512,64]{0,1:T(8,128)S(1)}, f32[512,64]{0,1:T(8,128)}, u32[]{:S(2)}) copy-start(f32[512,64]{0,1:T(8,128)} %param.3) | copy-start | bytes 393220
  397.7 1.8 collective-permute-start
  399.6 4.6 %collective-permute-start.1 = (f32[160,128]{1,0:T(8,128)S(1)}, f32[160,128]{1,0:T(8,128)S(1)}, u32[]{:S(2)}, u32[]{:S(2)}) collective-permute-start(f32[160,128]{1,0:T(8,128)S(1)} %get-tuple-element.17), channel_id=1, source_target_pairs={{0,2},{1,3},{2,0},{3,1},{4,6},{5,7},{6,4},{7,5},{8,10},{9,11},{10,... | collective-permute-start | bytes 245768 | tf_op jit(solution)/shard_map/ppermute | solution.py:305
  401.0 5.2 %collective-permute-start.2 = (f32[160,128]{1,0:T(8,128)S(1)}, f32[160,128]{1,0:T(8,128)S(1)}, u32[]{:S(2)}, u32[]{:S(2)}) collective-permute-start(f32[160,128]{1,0:T(8,128)S(1)} %get-tuple-element.19), channel_id=1, source_target_pairs={{0,4},{1,5},{2,6},{3,7},{4,0},{5,1},{6,2},{7,3},{8,12},{9,13},{10,... | collective-permute-start | bytes 245768 | tf_op jit(solution)/shard_map/ppermute | solution.py:305
  402.4 5.3 %collective-permute-start.3 = (f32[160,128]{1,0:T(8,128)S(1)}, f32[160,128]{1,0:T(8,128)S(1)}, u32[]{:S(2)}, u32[]{:S(2)}) collective-permute-start(f32[160,128]{1,0:T(8,128)S(1)} %get-tuple-element.18), channel_id=1, source_target_pairs={{0,6},{1,7},{2,4},{3,5},{4,2},{5,3},{6,0},{7,1},{8,14},{9,15},{10,... | collective-permute-start | bytes 245768 | tf_op jit(solution)/shard_map/ppermute | solution.py:305
  407.8 4.5 %collective-permute-start.4 = (f32[160,128]{1,0:T(8,128)S(1)}, f32[160,128]{1,0:T(8,128)S(1)}, u32[]{:S(2)}, u32[]{:S(2)}) collective-permute-start(f32[160,128]{1,0:T(8,128)S(1)} %fusion.1), channel_id=1, source_target_pairs={{0,8},{8,0},{16,24},{24,16},{1,9},{9,1},{17,25},{25,17},{2,10},{10... | collective-permute-start | bytes 245768 | tf_op jit(solution)/shard_map/ppermute | solution.py:312
  407.9 7.3 %collective-permute-start.5 = (f32[160,128]{1,0:T(8,128)S(1)}, f32[160,128]{1,0:T(8,128)S(1)}, u32[]{:S(2)}, u32[]{:S(2)}) collective-permute-start(f32[160,128]{1,0:T(8,128)S(1)} %fusion.1), channel_id=1, source_target_pairs={{0,16},{8,24},{16,0},{24,8},{1,17},{9,25},{17,1},{25,9},{2,18},{10... | collective-permute-start | bytes 245768 | tf_op jit(solution)/shard_map/ppermute | solution.py:312
  410.3 6.3 %collective-permute-start.6 = (f32[160,128]{1,0:T(8,128)S(1)}, f32[160,128]{1,0:T(8,128)S(1)}, u32[]{:S(2)}, u32[]{:S(2)}) collective-permute-start(f32[160,128]{1,0:T(8,128)S(1)} %fusion.1), channel_id=1, source_target_pairs={{0,24},{8,16},{16,8},{24,0},{1,25},{9,17},{17,9},{25,1},{2,26},{10... | collective-permute-start | bytes 245768 | tf_op jit(solution)/shard_map/ppermute | solution.py:312
  416.7 4.5 %collective-permute-start.7 = (f32[160,128]{1,0:T(8,128)S(1)}, f32[160,128]{1,0:T(8,128)S(1)}, u32[]{:S(2)}, u32[]{:S(2)}) collective-permute-start(f32[160,128]{1,0:T(8,128)S(1)} %add_add_fusion.refs_2_), channel_id=1, source_target_pairs={{0,2},{1,3},{2,0},{3,1},{4,6},{5,7},{6,4},{7,5},{8,10},{9,11},{10,... | collective-permute-start | bytes 245768 | tf_op jit(solution)/shard_map/ppermute | solution.py:305
  417.2 4.4 %collective-permute-start.8 = (f32[160,128]{1,0:T(8,128)S(1)}, f32[160,128]{1,0:T(8,128)S(1)}, u32[]{:S(2)}, u32[]{:S(2)}) collective-permute-start(f32[160,128]{1,0:T(8,128)S(1)} %add_add_fusion.refs_2_), channel_id=1, source_target_pairs={{0,4},{1,5},{2,6},{3,7},{4,0},{5,1},{6,2},{7,3},{8,12},{9,13},{10,... | collective-permute-start | bytes 245768 | tf_op jit(solution)/shard_map/ppermute | solution.py:305
  417.7 5.3 %collective-permute-start.9 = (f32[160,128]{1,0:T(8,128)S(1)}, f32[160,128]{1,0:T(8,128)S(1)}, u32[]{:S(2)}, u32[]{:S(2)}) collective-permute-start(f32[160,128]{1,0:T(8,128)S(1)} %add_add_fusion.refs_2_), channel_id=1, source_target_pairs={{0,6},{1,7},{2,4},{3,5},{4,2},{5,3},{6,0},{7,1},{8,14},{9,15},{10,... | collective-permute-start | bytes 245768 | tf_op jit(solution)/shard_map/ppermute | solution.py:305
  420.2 3.0 collective-permute-start.10
  421.2 2.0 collective-permute-start.11
  421.7 1.5 collective-permute-start.12
  423.1 1.3 collective-permute-start.13

commit v5 on v4

v5 whole, which is shorter than its diff:
```python
import functools

import jax
import jax.numpy as jnp
from jax import lax
from jax.experimental import pallas as pl
from jax.experimental.pallas import tpu as pltpu
from jax.sharding import PartitionSpec as P

ITERS = 3
HIGHEST = lax.Precision.HIGHEST
MIB = 1024 * 1024
PIVOTS = 16
PROJECT_CELLS = 8


def split(matrix):
    high = matrix.astype(jnp.bfloat16)
    low = (matrix - high.astype(jnp.float32)).astype(jnp.bfloat16)
    return high, low


def nn(left, right, precision=None):
    return lax.dot_general(
        left, right, (((1,), (0,)), ((), ())), precision=precision,
        preferred_element_type=jnp.float32,
    )


def nt(left, right, precision=None):
    return lax.dot_general(
        left, right, (((1,), (1,)), ((), ())), precision=precision,
        preferred_element_type=jnp.float32,
    )


def largest_step(extent, most):
    step = min(extent, most)
    while extent % step:
        step -= 1
    return step


def cell_matrix(block_ref):
    sources, cells, planes, cells_y = block_ref.shape
    return jnp.concatenate(
        [block_ref[:, i].reshape(sources * planes, cells_y) for i in range(cells)], axis=1
    )


def lower_segments(count):
    below = [(i, j, half) for i in range(count) for j in range(i) for half in range(2)]
    return below + [(i, i, 1) for i in range(count)] + [(i, i, 0) for i in range(0, count, 2)]


def piece_sizes(cells):
    sizes, size = [], 4
    while cells:
        sizes.append(min(size, cells))
        cells -= sizes[-1]
        size = min(3 * size, 24)
    return sizes


def gram_pack_kernel(block_ref, *refs):
    parts, held_ref, total_ref, sems = refs[:-3], refs[-3], refs[-2], refs[-1]
    arrivals, first = [], 0
    for n, size in enumerate(piece_sizes(block_ref.shape[1])):
        view = (slice(None), pl.ds(first, size))
        copy = pltpu.make_async_copy(block_ref.at[view], held_ref.at[view], sems.at[n])
        copy.start()
        arrivals.append((copy, view))
        first += size
    rows, group = parts[0].shape
    planes_total = total_ref.shape[0]
    half = planes_total // 2 // group * group
    for n, (copy, view) in enumerate(arrivals):
        copy.wait()
        high, low = split(cell_matrix(held_ref.at[view]))
        mixed = nt(high, low * jnp.bfloat16(2))
        total_ref[...] = mixed if n == 0 else total_ref[...] + mixed
        total_ref[:half, :half] += nt(high[:half], high[:half])
        doubled = jnp.concatenate([high[:half] * jnp.bfloat16(2), high[half:]], axis=0)
        total_ref[half:, :] += nt(high[half:], doubled)
    for i in range(planes_total // group):
        for j in range(i + 1):
            here = pl.ds(i * group, group), pl.ds(j * group, group)
            there = pl.ds(j * group, group), pl.ds(i * group, group)
            total_ref[here] = 0.5 * (total_ref[here] + total_ref[there].T)
    my_inner = lax.rem(lax.axis_index("af"), len(parts))
    for place in range(len(parts)):

        @pl.when(my_inner == place)
        def _(place=place):
            for k, part_ref in enumerate(parts):
                start = (place + k) % len(parts) * rows
                copy_rows(part_ref, start, total_ref)


def copy_rows(part_ref, start, total_ref):
    group = part_ref.shape[1]
    half = group // 2
    segments = lower_segments(total_ref.shape[0] // group)

    def quarter(i, skip, size):
        first = i * group
        if first >= total_ref.shape[0]:
            return jnp.zeros((size, half), jnp.float32)
        return total_ref[first + skip : first + skip + size, first : first + half]

    done = 0
    while done < part_ref.shape[0]:
        n, skip = divmod(start + done, half)
        size = min(half - skip, part_ref.shape[0] - done)
        if n >= len(segments):
            value = jnp.zeros((size, group), jnp.float32)
        else:
            i, j, lower = segments[n]
            if i == j and not lower:
                value = jnp.concatenate([quarter(i, skip, size), quarter(i + 1, skip, size)], axis=1)
            else:
                first = i * group + lower * half + skip
                value = total_ref[first : first + size, j * group : (j + 1) * group]
        part_ref[done : done + size, :] = value
        done += size


def gram_pack(block, parts, devices):
    planes_total = block.shape[0] * block.shape[2]
    group = planes_total // largest_step(planes_total, planes_total // 128)
    rows = len(lower_segments(planes_total // group)) * (group // 2)
    rows += -rows % (8 * devices)
    vmem = pl.BlockSpec(memory_space=pltpu.VMEM)
    return pl.pallas_call(
        gram_pack_kernel,
        in_specs=[pl.BlockSpec(memory_space=pl.ANY)],
        out_specs=[vmem] * parts,
        out_shape=[jax.ShapeDtypeStruct((rows // parts, group), jnp.float32)] * parts,
        scratch_shapes=[
            pltpu.VMEM(block.shape, jnp.float32),
            pltpu.VMEM((planes_total, planes_total), jnp.float32),
            pltpu.SemaphoreType.DMA((len(piece_sizes(block.shape[1])),)),
        ],
        compiler_params=pltpu.CompilerParams(vmem_limit_bytes=48 * MIB),
        name="gram_pack",
    )(block)


def inverse_cholesky(matrix):
    size = matrix.shape[0]
    step = largest_step(size, PIVOTS)
    ones = lax.broadcasted_iota(jnp.int32, (size, size), 0) == lax.broadcasted_iota(
        jnp.int32, (size, size), 1
    )
    work = jnp.concatenate([matrix, ones.astype(jnp.float32)], axis=1)
    work = [work[first : first + step] for first in range(0, size, step)]
    shape = work[0].shape
    rows = lax.broadcasted_iota(jnp.int32, shape, 0)
    done = []
    for n in range(len(work)):
        scale = jnp.zeros(shape, jnp.float32)
        columns = {
            m: [
                jnp.broadcast_to(work[m][:, lane : lane + 1], shape)
                for lane in range(n * step, (n + 1) * step)
            ]
            for m in range(n, len(work))
        }
        for i in range(step):
            pivot = columns[n][i][i : i + 1]
            scale = jnp.where(rows == i, lax.rsqrt(pivot), scale)
            inverse = 1.0 / pivot
            row = work[n][i : i + 1] * inverse
            others = [columns[n][k][i : i + 1] * inverse for k in range(i + 1, step)]
            for m in range(n, len(work)):
                factor = columns[m][i]
                if m == n:
                    factor = jnp.where(rows > i, factor, 0.0)
                work[m] = work[m] - factor * row
                for k, other in enumerate(others):
                    columns[m][i + 1 + k] = columns[m][i + 1 + k] - factor * other
        done.append(work[n] * scale)
    return jnp.concatenate(done, axis=0)[:, size:]


def split_three(matrix):
    high, low = split(matrix)
    rest = matrix - high.astype(jnp.float32) - low.astype(jnp.float32)
    return high, low, rest.astype(jnp.bfloat16)


def iterate(matrix, subspace):
    matrix_high, matrix_low, matrix_rest = split_three(matrix)
    rank = subspace.shape[0]
    for _ in range(ITERS):
        high, low, rest = split_three(subspace)
        by_high = nn(jnp.concatenate([high, low, rest], axis=0), matrix_high)
        by_low = nn(jnp.concatenate([high, low], axis=0), matrix_low)
        small = by_high[2 * rank :] + by_low[rank:] + nn(high, matrix_rest)
        product = by_high[:rank] + (by_high[rank : 2 * rank] + by_low[:rank] + small)
        inverse = inverse_cholesky(nt(product, product, HIGHEST))
        subspace = nn(inverse, product, HIGHEST)
    return subspace


def unpack(places, pieces, packed_ref, gram_ref):
    rows, group = pieces[0].shape
    for n, piece in enumerate(pieces):
        packed_ref[pl.ds(pl.multiple_of(places[n] * rows, 8), rows), :] = piece[...]
    half = group // 2
    for n, (i, j, lower) in enumerate(lower_segments(gram_ref.shape[0] // group)):
        segment = packed_ref[n * half : (n + 1) * half, :]
        rows_here = pl.ds(i * group + lower * half, half)
        if i != j:
            gram_ref[rows_here, j * group : (j + 1) * group] = segment
            mirrored = pl.ds(i * group + lower * half, half)
            gram_ref[j * group : (j + 1) * group, mirrored] = segment.T
        elif lower:
            gram_ref[rows_here, i * group : (i + 1) * group] = segment
            gram_ref[i * group : i * group + half, i * group + half : (i + 1) * group] = (
                segment[:, :half].T
            )
        else:
            for k in range(2):
                first = (i + k) * group
                if first < gram_ref.shape[0]:
                    gram_ref[first : first + half, first : first + half] = (
                        segment[:, k * half : (k + 1) * half]
                    )


def finish_kernel(pieces_count, blocks_count, *refs):
    basis_ref = refs[0]
    pieces = refs[1 : 1 + pieces_count]
    blocks = refs[1 + pieces_count : 1 + pieces_count + blocks_count]
    rest = refs[1 + pieces_count + blocks_count :]
    out_ref, packed_ref, gram_ref, result_ref, in_sems, out_sems = rest[:1] + rest[1:4] + rest[-2:]
    held = rest[4:-2]
    steps, first = [], 0
    for n, block in enumerate(blocks):
        for start in range(0, block.shape[1], PROJECT_CELLS):
            size = min(PROJECT_CELLS, block.shape[1] - start)
            cells = (slice(None), pl.ds(start, size))
            copy = pltpu.make_async_copy(
                block.at[cells], held[n].at[cells], in_sems.at[len(steps)]
            )
            copy.start()
            steps.append((held[n].at[cells], pl.ds(first, size), copy))
            first += size
    unpack(piece_places(), pieces, packed_ref, gram_ref)
    subspace = iterate(gram_ref[...], basis_ref[...])
    rank = subspace.shape[0]
    basis_high, basis_low = split(subspace)
    both = jnp.concatenate([basis_high, basis_low], axis=0)
    copies = []
    for n, (block, cells, arrival) in enumerate(steps):
        arrival.wait()
        cells_y = block.shape[3]
        high, low = split(cell_matrix(block))
        main = nn(both, high)
        result = main[:rank] + (main[rank:] + nn(basis_high, low))
        for i in range(cells.size):
            result_ref[cells.start + i] = result[:, i * cells_y : (i + 1) * cells_y]
        copy = pltpu.make_async_copy(result_ref.at[cells], out_ref.at[cells], out_sems.at[n])
        copy.start()
        copies.append(copy)
    for copy in copies:
        copy.wait()


def finish(pieces, basis_t, blocks):
    rank, planes_total = basis_t.shape
    cells = sum(block.shape[1] for block in blocks)
    cells_y = blocks[0].shape[3]
    rows, group = pieces[0].shape
    steps = sum(pl.cdiv(block.shape[1], PROJECT_CELLS) for block in blocks)
    vmem = pl.BlockSpec(memory_space=pltpu.VMEM)
    anywhere = pl.BlockSpec(memory_space=pl.ANY)
    out_shape = (cells, rank, cells_y)
    return pl.pallas_call(
        functools.partial(finish_kernel, len(pieces), len(blocks)),
        in_specs=[vmem] * (1 + len(pieces))
        + [anywhere] * len(blocks),
        out_specs=anywhere,
        out_shape=jax.ShapeDtypeStruct(out_shape, jnp.float32),
        scratch_shapes=[
            pltpu.VMEM((rows * len(pieces), group), jnp.float32),
            pltpu.VMEM((planes_total, planes_total), jnp.float32),
            pltpu.VMEM(out_shape, jnp.float32),
        ]
        + [pltpu.VMEM(block.shape, jnp.float32) for block in blocks]
        + [pltpu.SemaphoreType.DMA((steps,)), pltpu.SemaphoreType.DMA((steps,))],
        compiler_params=pltpu.CompilerParams(vmem_limit_bytes=56 * MIB),
        name="finish",
    )(basis_t, *pieces, *blocks)


def toward(i, step, count):
    return i ^ step if count & (count - 1) == 0 else (i + step) % count


def origin(i, step, count):
    return i ^ step if count & (count - 1) == 0 else (i - step) % count


def inner_size():
    return 2 if lax.axis_size("af") % 2 == 0 else 1


def af_place():
    inner = inner_size()
    me = lax.axis_index("af")
    return lax.div(me, inner), lax.rem(me, inner), lax.axis_size("af") // inner


def piece_places():
    my_outer, my_inner, outer = af_place()
    places = []
    for i in range(inner_size()):
        group = my_inner if i == 0 else 1 - my_inner
        places += [group * outer + origin(my_outer, k, outer) for k in range(outer)]
    return places


def cut_kernel(kept_ref, came_ref, *refs):
    outs, total_ref = refs[:-1], refs[-1]
    my_outer, _, outer = af_place()
    total_ref[...] = kept_ref[...] + came_ref[...]
    rows = outs[0].shape[0]
    for k, out_ref in enumerate(outs):
        start = toward(my_outer, k, outer) * rows
        out_ref[...] = total_ref[pl.ds(pl.multiple_of(start, 8), rows), :]


def cut(kept, came, outer):
    rows, group = kept.shape
    vmem = pl.BlockSpec(memory_space=pltpu.VMEM)
    return pl.pallas_call(
        cut_kernel,
        in_specs=[vmem] * 2,
        out_specs=[vmem] * outer,
        out_shape=[jax.ShapeDtypeStruct((rows // outer, group), jnp.float32)] * outer,
        scratch_shapes=[pltpu.VMEM(kept.shape, jnp.float32)],
        compiler_params=pltpu.CompilerParams(vmem_limit_bytes=8 * MIB),
        name="cut",
    )(kept, came)


def sum_over_devices(parts):
    groups_af, groups_ta = lax.axis_size("af"), lax.axis_size("ta")
    inner = inner_size()
    outer = groups_af // inner

    def to_inner(array):
        return lax.ppermute(array, "af", [(i, i ^ 1) for i in range(groups_af)])

    def to_outer(array, step):
        return lax.ppermute(
            array,
            "af",
            [(i, toward(i // inner, step, outer) * inner + i % inner) for i in range(groups_af)],
        )

    def to_ta(array, step):
        return lax.ppermute(array, "ta", [(i, toward(i, step, groups_ta)) for i in range(groups_ta)])

    def total(arrays):
        return functools.reduce(jnp.add, arrays)

    came = to_inner(parts[1]) if inner == 2 else jnp.zeros_like(parts[0])
    parts = cut(parts[0], came, outer)
    mine = total([parts[0]] + [to_outer(parts[k], k) for k in range(1, outer)])
    mine = total([mine] + [to_ta(mine, k) for k in range(1, groups_ta)])
    pieces = [mine] + [to_outer(mine, k) for k in range(1, outer)]
    if inner == 2:
        pieces += [to_inner(piece) for piece in pieces]
    return pieces


def arrange_kernel(spots, in_ref, out_ref, held_ref, ready_ref, in_sems, out_sems):
    part, targets = held_ref.shape[3], held_ref.shape[2]
    arrivals, sent = [], []
    for n, (frame, x, _, _) in enumerate(spots):
        copy = pltpu.make_async_copy(
            in_ref.at[frame, :, :, pl.ds(x, part)], held_ref.at[n], in_sems.at[n]
        )
        copy.start()
        arrivals.append(copy)
    for n, (_, _, group, cell) in enumerate(spots):
        arrivals[n].wait()
        for target in range(targets):
            ready_ref[n, target] = jnp.swapaxes(held_ref[n, :, target], 0, 1)
        copy = pltpu.make_async_copy(
            ready_ref.at[n],
            out_ref.at[pl.ds(group * targets, targets), pl.ds(cell, part)],
            out_sems.at[n],
        )
        copy.start()
        sent.append(copy)
    for copy in sent:
        copy.wait()


def outgoing(velocity):
    groups_ta, groups_af = lax.axis_size("ta"), lax.axis_size("af")
    frames, planes, cells_x, cells_y = velocity.shape
    block_frames, block_x = frames // groups_ta, cells_x // groups_af
    cells = block_frames * block_x
    if planes % 8 or block_x % 8:
        ordered = velocity.reshape(groups_ta, block_frames, planes, groups_af, block_x, cells_y)
        ordered = ordered.transpose(0, 3, 1, 4, 2, 5)
        return ordered.reshape(groups_ta * groups_af, cells, planes, cells_y)
    spots = [
        (group * block_frames + frame, 0, group, frame * block_x)
        for group in range(groups_ta)
        for frame in range(block_frames)
    ]
    anywhere = pl.BlockSpec(memory_space=pl.ANY)
    return pl.pallas_call(
        functools.partial(arrange_kernel, spots),
        in_specs=[anywhere],
        out_specs=anywhere,
        out_shape=pltpu.HBM((groups_ta * groups_af, cells, planes, cells_y), jnp.float32),
        scratch_shapes=[
            pltpu.VMEM((len(spots), planes, groups_af, block_x, cells_y), jnp.float32),
            pltpu.VMEM((len(spots), groups_af, block_x, planes, cells_y), jnp.float32),
            pltpu.SemaphoreType.DMA((len(spots),)),
            pltpu.SemaphoreType.DMA((len(spots),)),
        ],
        compiler_params=pltpu.CompilerParams(vmem_limit_bytes=56 * MIB),
        name="arrange",
    )(velocity.reshape(frames, planes, groups_af, block_x, cells_y))


def local(velocity, initial_basis):
    groups_ta, groups_af = lax.axis_size("ta"), lax.axis_size("af")
    frames, planes, cells_x, cells_y = velocity.shape
    block_frames, block_x = frames // groups_ta, cells_x // groups_af
    block = lax.all_to_all(
        outgoing(velocity), ("ta", "af"), split_axis=0, concat_axis=0, tiled=True
    )
    if planes % 8:
        block = block.transpose(1, 0, 2, 3).reshape(1, block.shape[1], -1, cells_y)
    inner = inner_size()
    pieces = sum_over_devices(gram_pack(block, inner, groups_af))
    core = finish(pieces, initial_basis.T, [block])
    return core.reshape(block_frames, block_x, core.shape[1], cells_y)


def solution(mesh):
    placed = (P(None, ("ta", "af"), None, None), P())
    return jax.shard_map(
        local, mesh=mesh, in_specs=placed, out_specs=P("ta", "af", None, None), check_vma=False
    )
```

time: 440 us -> 435 us (0.989)
  blocking collectives: 0 us -> 371 us
  waiting for transfers between devices: 368 us -> 14.5 us
  starting transfers between devices: 26.5 us -> 11.7 us
  Pallas kernels: 45.3 us -> 37 us
    all_to_all x0 -> x1, blocking collectives: none -> 371 us  [local(): lax.all_to_all(outgoing(velocity), ('ta', 'af'), split_axis=0, concat_axi...]
    all_to_all x3 -> x0, waiting for transfers between devices: 353 us -> none  [local(): lax.all_to_all(block, ('ta', 'af'), split_axis=0, concat_axis=0, tiled=True)]
    all_to_all x3 -> x0, starting transfers between devices: 14.9 us -> none  [local(): lax.all_to_all(block, ('ta', 'af'), split_axis=0, concat_axis=0, tiled=True)]
    pallas_call x3 -> x2, Pallas kernels: 15.5 us -> 11.5 us  [the longest x1 11.4 us: gram_pack(): pl.pallas_call(gram_pack_kernel, in_specs=[pl.BlockSpec(memory_space=pl.A...]
    pallas_call x3 -> x1, Pallas kernels: 14.4 us -> 12 us  [outgoing(): pl.pallas_call(functools.partial(arrange_kernel, spots), in_specs=[anywhe...]
  transfers between devices with their start and end apart: 17 -> 14, of which waited for: 14 -> 12; matrix products, arithmetic and copies ran while one was open for 0% -> 0% of each run, Pallas kernels for 5% -> 0%
where the time goes in v5:
time: 435 us
  blocking collectives  371 us (85%)
  Pallas kernels  37 us (9%)
  waiting for transfers between devices  14.5 us (3%)
  starting transfers between devices  11.7 us (3%)
    all_to_all x1, blocking collectives, local(): lax.all_to_all(outgoing(velocity), ('ta', 'af'), split_axis=0, concat_axi...  371 us
    pallas_call x1, Pallas kernels, finish(): pl.pallas_call(functools.partial(finish_kernel, len(pieces), len(blocks))...  13.5 us
    pallas_call x1, Pallas kernels, outgoing(): pl.pallas_call(functools.partial(arrange_kernel, spots), in_specs=[anywhe...  12 us
    pallas_call x1, Pallas kernels, gram_pack(): pl.pallas_call(gram_pack_kernel, in_specs=[pl.BlockSpec(memory_space=pl.A...  11.4 us
  transfers between devices with their start and end apart: 14, of which 12 were waited for; matrix products, arithmetic and copies ran while one was open for 0% of the time, Pallas kernels for 0%

profile of v5, /device:TPU:0, one launch (start us, length us, event | category | flops | bytes accessed | tf_op | source)
XLA Modules:
  0.0 434.8 jit_solution(13187074731255823)
XLA Ops:
  0.0 12.0 %arrange.1 = f32[32,64,16,128]{3,2,1,0:T(8,128)} custom-call(f32[16,16,8,16,128]{4,3,2,1,0:T(8,128)} %bitcast.3), custom_call_target="tpu_custom_call" | custom-call | tf_op jit(solution)/shard_map/arrange/pallas_call | solution.py:419
  12.1 370.7 %all_to_all.5.block_ref.refs_9_ = f32[32,64,16,128]{3,2,1,0:T(8,128)} all-to-all(f32[32,64,16,128]{3,2,1,0:T(8,128)} %arrange.1), channel_id=1, replica_groups=mesh['ta'=4,'af'=8] {'ta','af'}, dimensions={0} | all-to-all | bytes 33554432 | tf_op jit(solution)/shard_map/all_to_all | solution.py:439
  382.8 11.4 %gram_pack.1 = (f32[576,128]{1,0:T(8,128)S(1)}, f32[576,128]{1,0:T(8,128)S(1)}) custom-call(f32[32,64,16,128]{3,2,1,0:T(8,128)} %all_to_all.5.block_ref.refs_9_), custom_call_target="tpu_custom_call" | custom-call | tf_op jit(solution)/shard_map/gram_pack/pallas_call | solution.py:134
  394.3 1.6 collective-permute-done.came_ref
  395.9 1.8 collective-permute-start.1
  397.7 1.3 collective-permute-start.2
  398.9 0.5 collective-permute-start.3
  399.4 0.9 collective-permute-done.1
  400.3 1.7 collective-permute-done.2
  402.0 2.1 collective-permute-done.3
  404.2 2.1 collective-permute-start.6
  406.3 2.4 collective-permute-start.4
  408.6 2.1 collective-permute-done.6
  410.7 1.9 collective-permute-done.5
  412.6 1.1 collective-permute-start.9
  413.7 1.2 collective-permute-start.8
  414.9 1.3 collective-permute-start.7
  416.2 2.0 collective-permute-done.9.refs_4_
  418.1 0.7 collective-permute-done.8.refs_3_
  418.8 0.4 collective-permute-done.7.refs_2_
  419.4 0.7 collective-permute-done.12.refs_7_
  420.1 0.4 collective-permute-done.11.refs_6_
  420.7 0.4 copy-done.7
  421.1 13.5 %finish.1 = f32[64,64,128]{2,1,0:T(8,128)} custom-call(f32[64,512]{1,0:T(8,128)} %bitcast.4, f32[144,128]{1,0:T(8,128)} %copy-done, f32[144,128]{1,0:T(8,128)} %copy-done.3, f32[144,128]{1,0:T(8,128)} %copy-done.2, f32[144,128]{1,0:T(8,128)} %copy-done.1, f32[144,128]{1,0:T(8,128)} %copy-done.4, f32[144,128]{1,0:T(8,128)} %copy-done.7, ...), custom_call_target="tpu_custom_call" | custom-call | tf_op jit(solution)/shard_map/finish/pallas_call | solution.py:280
  (27 shorter events, 0.5 us)
Async XLA Ops:
  394.2 1.6 collective-permute-start
  395.9 4.4 %collective-permute-start.1 = (f32[144,128]{1,0:T(8,128)S(1)}, f32[144,128]{1,0:T(8,128)S(1)}, u32[]{:S(2)}, u32[]{:S(2)}) collective-permute-start(f32[144,128]{1,0:T(8,128)S(1)} %get-tuple-element.14), channel_id=1, source_target_pairs={{0,2},{1,3},{2,0},{3,1},{4,6},{5,7},{6,4},{7,5},{8,10},{9,11},{10,... | collective-permute-start | bytes 221192 | tf_op jit(solution)/shard_map/ppermute | solution.py:358
  397.7 4.4 %collective-permute-start.2 = (f32[144,128]{1,0:T(8,128)S(1)}, f32[144,128]{1,0:T(8,128)S(1)}, u32[]{:S(2)}, u32[]{:S(2)}) collective-permute-start(f32[144,128]{1,0:T(8,128)S(1)} %get-tuple-element.15), channel_id=1, source_target_pairs={{0,4},{1,5},{2,6},{3,7},{4,0},{5,1},{6,2},{7,3},{8,12},{9,13},{10,... | collective-permute-start | bytes 221192 | tf_op jit(solution)/shard_map/ppermute | solution.py:358
  398.9 5.3 %collective-permute-start.3 = (f32[144,128]{1,0:T(8,128)S(1)}, f32[144,128]{1,0:T(8,128)S(1)}, u32[]{:S(2)}, u32[]{:S(2)}) collective-permute-start(f32[144,128]{1,0:T(8,128)S(1)} %get-tuple-element.16), channel_id=1, source_target_pairs={{0,6},{1,7},{2,4},{3,5},{4,2},{5,3},{6,0},{7,1},{8,14},{9,15},{10,... | collective-permute-start | bytes 221192 | tf_op jit(solution)/shard_map/ppermute | solution.py:358
  404.2 6.5 %collective-permute-start.6 = (f32[144,128]{1,0:T(8,128)S(1)}, f32[144,128]{1,0:T(8,128)S(1)}, u32[]{:S(2)}, u32[]{:S(2)}) collective-permute-start(f32[144,128]{1,0:T(8,128)S(1)} %add_add_fusion.1), channel_id=1, source_target_pairs={{0,24},{8,16},{16,8},{24,0},{1,25},{9,17},{17,9},{25,1},{2,26},{10... | collective-permute-start | bytes 221192 | tf_op jit(solution)/shard_map/ppermute | solution.py:365
  406.3 6.3 %collective-permute-start.5 = (f32[144,128]{1,0:T(8,128)S(1)}, f32[144,128]{1,0:T(8,128)S(1)}, u32[]{:S(2)}, u32[]{:S(2)}) collective-permute-start(f32[144,128]{1,0:T(8,128)S(1)} %add_add_fusion.1), channel_id=1, source_target_pairs={{0,16},{8,24},{16,0},{24,8},{1,17},{9,25},{17,1},{25,9},{2,18},{10... | collective-permute-start | bytes 221192 | tf_op jit(solution)/shard_map/ppermute | solution.py:365
  406.3 6.3 %collective-permute-start.4 = (f32[144,128]{1,0:T(8,128)S(1)}, f32[144,128]{1,0:T(8,128)S(1)}, u32[]{:S(2)}, u32[]{:S(2)}) collective-permute-start(f32[144,128]{1,0:T(8,128)S(1)} %add_add_fusion.1), channel_id=1, source_target_pairs={{0,8},{8,0},{16,24},{24,16},{1,9},{9,1},{17,25},{25,17},{2,10},{10... | collective-permute-start | bytes 221192 | tf_op jit(solution)/shard_map/ppermute | solution.py:365
  412.6 7.9 %copy-start = (f32[144,128]{1,0:T(8,128)}, f32[144,128]{1,0:T(8,128)S(1)}, u32[]{:S(2)}) copy-start(f32[144,128]{1,0:T(8,128)S(1)} %add_add_fusion.refs_1_) | copy-start | bytes 221188
  412.6 5.5 %collective-permute-start.9 = (f32[144,128]{1,0:T(8,128)S(1)}, f32[144,128]{1,0:T(8,128)S(1)}, u32[]{:S(2)}, u32[]{:S(2)}) collective-permute-start(f32[144,128]{1,0:T(8,128)S(1)} %add_add_fusion.refs_1_), channel_id=1, source_target_pairs={{0,6},{1,7},{2,4},{3,5},{4,2},{5,3},{6,0},{7,1},{8,14},{9,15},{10,... | collective-permute-start | bytes 221192 | tf_op jit(solution)/shard_map/ppermute | solution.py:358
  413.7 5.1 %collective-permute-start.8 = (f32[144,128]{1,0:T(8,128)S(1)}, f32[144,128]{1,0:T(8,128)S(1)}, u32[]{:S(2)}, u32[]{:S(2)}) collective-permute-start(f32[144,128]{1,0:T(8,128)S(1)} %add_add_fusion.refs_1_), channel_id=1, source_target_pairs={{0,4},{1,5},{2,6},{3,7},{4,0},{5,1},{6,2},{7,3},{8,12},{9,13},{10,... | collective-permute-start | bytes 221192 | tf_op jit(solution)/shard_map/ppermute | solution.py:358
  414.9 4.4 %collective-permute-start.7 = (f32[144,128]{1,0:T(8,128)S(1)}, f32[144,128]{1,0:T(8,128)S(1)}, u32[]{:S(2)}, u32[]{:S(2)}) collective-permute-start(f32[144,128]{1,0:T(8,128)S(1)} %add_add_fusion.refs_1_), channel_id=1, source_target_pairs={{0,2},{1,3},{2,0},{3,1},{4,6},{5,7},{6,4},{7,5},{8,10},{9,11},{10,... | collective-permute-start | bytes 221192 | tf_op jit(solution)/shard_map/ppermute | solution.py:358
  416.2 3.2 collective-permute-start.10
  418.1 2.4 copy-start.1
  418.1 1.3 collective-permute-start.13
  418.8 1.7 copy-start.2
  418.8 1.3 collective-permute-start.12
  419.2 1.3 copy-start.3
  419.2 1.3 collective-permute-start.11
  419.3 1.2 copy-start.4
  419.4 1.1 copy-start.5
  420.1 0.6 copy-start.6
  420.5 0.6 copy-start.7

commit v6 on v5

--- a/solution.py
+++ b/solution.py
@@ -377,28 +377,21 @@
     return pieces
 
 
-def arrange_kernel(spots, in_ref, out_ref, held_ref, ready_ref, in_sems, out_sems):
+def arrange_kernel(spots, in_ref, out_ref, held_ref, sems):
     part, targets = held_ref.shape[3], held_ref.shape[2]
-    arrivals, sent = [], []
+    arrivals = []
     for n, (frame, x, _, _) in enumerate(spots):
         copy = pltpu.make_async_copy(
-            in_ref.at[frame, :, :, pl.ds(x, part)], held_ref.at[n], in_sems.at[n]
+            in_ref.at[frame, :, :, pl.ds(x, part)], held_ref.at[n], sems.at[n]
         )
         copy.start()
         arrivals.append(copy)
     for n, (_, _, group, cell) in enumerate(spots):
         arrivals[n].wait()
         for target in range(targets):
-            ready_ref[n, target] = jnp.swapaxes(held_ref[n, :, target], 0, 1)
-        copy = pltpu.make_async_copy(
-            ready_ref.at[n],
-            out_ref.at[pl.ds(group * targets, targets), pl.ds(cell, part)],
-            out_sems.at[n],
-        )
-        copy.start()
-        sent.append(copy)
-    for copy in sent:
-        copy.wait()
+            out_ref[group * targets + target, cell : cell + part] = jnp.swapaxes(
+                held_ref[n, :, target], 0, 1
+            )
 
 
 def outgoing(velocity):
@@ -419,15 +412,15 @@
     return pl.pallas_call(
         functools.partial(arrange_kernel, spots),
         in_specs=[anywhere],
-        out_specs=anywhere,
-        out_shape=pltpu.HBM((groups_ta * groups_af, cells, planes, cells_y), jnp.float32),
+        out_specs=pl.BlockSpec(memory_space=pltpu.VMEM),
+        out_shape=jax.ShapeDtypeStruct(
+            (groups_ta * groups_af, cells, planes, cells_y), jnp.float32
+        ),
         scratch_shapes=[
             pltpu.VMEM((len(spots), planes, groups_af, block_x, cells_y), jnp.float32),
-            pltpu.VMEM((len(spots), groups_af, block_x, planes, cells_y), jnp.float32),
-            pltpu.SemaphoreType.DMA((len(spots),)),
             pltpu.SemaphoreType.DMA((len(spots),)),
         ],
-        compiler_params=pltpu.CompilerParams(vmem_limit_bytes=56 * MIB),
+        compiler_params=pltpu.CompilerParams(vmem_limit_bytes=30 * MIB),
         name="arrange",
     )(velocity.reshape(frames, planes, groups_af, block_x, cells_y))
 

time: 435 us -> 429 us (0.986)
  Pallas kernels: 37 us -> 31 us
    pallas_call x1, Pallas kernels: 12 us -> 6.12 us  [outgoing(): pl.pallas_call(functools.partial(arrange_kernel, spots), in_specs=[anywhe...]
where the time goes in v6:
time: 429 us
  blocking collectives  371 us (86%)
  Pallas kernels  31 us (7%)
  waiting for transfers between devices  14.5 us (3%)
  starting transfers between devices  11.7 us (3%)
    all_to_all x1, blocking collectives, local(): lax.all_to_all(outgoing(velocity), ('ta', 'af'), split_axis=0, concat_axi...  371 us
    pallas_call x1, Pallas kernels, finish(): pl.pallas_call(functools.partial(finish_kernel, len(pieces), len(blocks))...  13.4 us
    pallas_call x1, Pallas kernels, gram_pack(): pl.pallas_call(gram_pack_kernel, in_specs=[pl.BlockSpec(memory_space=pl.A...  11.4 us
  transfers between devices with their start and end apart: 14, of which 12 were waited for; matrix products, arithmetic and copies ran while one was open for 0% of the time, Pallas kernels for 0%

profile of v6, /device:TPU:0, one launch (start us, length us, event | category | flops | bytes accessed | tf_op | source)
XLA Modules:
  0.0 428.6 jit_solution(4019891669313735545)
XLA Ops:
  0.0 6.1 %arrange.1 = f32[32,64,16,128]{3,2,1,0:T(8,128)S(1)} custom-call(f32[16,16,8,16,128]{4,3,2,1,0:T(8,128)} %bitcast.3), custom_call_target="tpu_custom_call" | custom-call | tf_op jit(solution)/shard_map/arrange/pallas_call | solution.py:412
  6.1 370.5 %all_to_all.5.block_ref.refs_9_ = f32[32,64,16,128]{3,2,1,0:T(8,128)} all-to-all(f32[32,64,16,128]{3,2,1,0:T(8,128)S(1)} %arrange.1), channel_id=1, replica_groups=mesh['ta'=4,'af'=8] {'ta','af'}, dimensions={0} | all-to-all | bytes 33554432 | tf_op jit(solution)/shard_map/all_to_all | solution.py:432
  376.6 11.4 %gram_pack.1 = (f32[576,128]{1,0:T(8,128)S(1)}, f32[576,128]{1,0:T(8,128)S(1)}) custom-call(f32[32,64,16,128]{3,2,1,0:T(8,128)} %all_to_all.5.block_ref.refs_9_), custom_call_target="tpu_custom_call" | custom-call | tf_op jit(solution)/shard_map/gram_pack/pallas_call | solution.py:134
  388.1 1.6 collective-permute-done.came_ref
  389.7 1.8 collective-permute-start.1
  391.5 1.3 collective-permute-start.2
  392.8 0.5 collective-permute-start.3
  393.3 0.9 collective-permute-done.1
  394.2 1.7 collective-permute-done.2
  395.9 2.1 collective-permute-done.3
  398.0 2.1 collective-permute-start.6
  400.1 2.4 collective-permute-start.4
  402.5 2.1 collective-permute-done.6
  404.6 1.8 collective-permute-done.5
  406.5 1.1 collective-permute-start.9
  407.5 1.2 collective-permute-start.8
  408.8 1.3 collective-permute-start.7
  410.0 1.9 collective-permute-done.9.refs_4_
  412.0 0.7 collective-permute-done.8.refs_3_
  412.7 0.4 collective-permute-done.7.refs_2_
  413.3 0.7 collective-permute-done.12.refs_7_
  413.9 0.4 collective-permute-done.11.refs_6_
  414.6 0.4 copy-done.7
  415.0 13.4 %finish.1 = f32[64,64,128]{2,1,0:T(8,128)} custom-call(f32[64,512]{1,0:T(8,128)} %bitcast.4, f32[144,128]{1,0:T(8,128)} %copy-done, f32[144,128]{1,0:T(8,128)} %copy-done.3, f32[144,128]{1,0:T(8,128)} %copy-done.2, f32[144,128]{1,0:T(8,128)} %copy-done.1, f32[144,128]{1,0:T(8,128)} %copy-done.4, f32[144,128]{1,0:T(8,128)} %copy-done.7, ...), custom_call_target="tpu_custom_call" | custom-call | tf_op jit(solution)/shard_map/finish/pallas_call | solution.py:280
  (27 shorter events, 0.5 us)
Async XLA Ops:
  388.0 1.6 collective-permute-start
  389.7 4.4 %collective-permute-start.1 = (f32[144,128]{1,0:T(8,128)S(1)}, f32[144,128]{1,0:T(8,128)S(1)}, u32[]{:S(2)}, u32[]{:S(2)}) collective-permute-start(f32[144,128]{1,0:T(8,128)S(1)} %get-tuple-element.14), channel_id=1, source_target_pairs={{0,2},{1,3},{2,0},{3,1},{4,6},{5,7},{6,4},{7,5},{8,10},{9,11},{10,... | collective-permute-start | bytes 221192 | tf_op jit(solution)/shard_map/ppermute | solution.py:358
  391.5 4.4 %collective-permute-start.2 = (f32[144,128]{1,0:T(8,128)S(1)}, f32[144,128]{1,0:T(8,128)S(1)}, u32[]{:S(2)}, u32[]{:S(2)}) collective-permute-start(f32[144,128]{1,0:T(8,128)S(1)} %get-tuple-element.15), channel_id=1, source_target_pairs={{0,4},{1,5},{2,6},{3,7},{4,0},{5,1},{6,2},{7,3},{8,12},{9,13},{10,... | collective-permute-start | bytes 221192 | tf_op jit(solution)/shard_map/ppermute | solution.py:358
  392.8 5.3 %collective-permute-start.3 = (f32[144,128]{1,0:T(8,128)S(1)}, f32[144,128]{1,0:T(8,128)S(1)}, u32[]{:S(2)}, u32[]{:S(2)}) collective-permute-start(f32[144,128]{1,0:T(8,128)S(1)} %get-tuple-element.16), channel_id=1, source_target_pairs={{0,6},{1,7},{2,4},{3,5},{4,2},{5,3},{6,0},{7,1},{8,14},{9,15},{10,... | collective-permute-start | bytes 221192 | tf_op jit(solution)/shard_map/ppermute | solution.py:358
  398.0 6.6 %collective-permute-start.6 = (f32[144,128]{1,0:T(8,128)S(1)}, f32[144,128]{1,0:T(8,128)S(1)}, u32[]{:S(2)}, u32[]{:S(2)}) collective-permute-start(f32[144,128]{1,0:T(8,128)S(1)} %add_add_fusion.1), channel_id=1, source_target_pairs={{0,24},{8,16},{16,8},{24,0},{1,25},{9,17},{17,9},{25,1},{2,26},{10... | collective-permute-start | bytes 221192 | tf_op jit(solution)/shard_map/ppermute | solution.py:365
  400.1 6.3 %collective-permute-start.5 = (f32[144,128]{1,0:T(8,128)S(1)}, f32[144,128]{1,0:T(8,128)S(1)}, u32[]{:S(2)}, u32[]{:S(2)}) collective-permute-start(f32[144,128]{1,0:T(8,128)S(1)} %add_add_fusion.1), channel_id=1, source_target_pairs={{0,16},{8,24},{16,0},{24,8},{1,17},{9,25},{17,1},{25,9},{2,18},{10... | collective-permute-start | bytes 221192 | tf_op jit(solution)/shard_map/ppermute | solution.py:365
  400.1 6.3 %collective-permute-start.4 = (f32[144,128]{1,0:T(8,128)S(1)}, f32[144,128]{1,0:T(8,128)S(1)}, u32[]{:S(2)}, u32[]{:S(2)}) collective-permute-start(f32[144,128]{1,0:T(8,128)S(1)} %add_add_fusion.1), channel_id=1, source_target_pairs={{0,8},{8,0},{16,24},{24,16},{1,9},{9,1},{17,25},{25,17},{2,10},{10... | collective-permute-start | bytes 221192 | tf_op jit(solution)/shard_map/ppermute | solution.py:365
  406.5 7.9 %copy-start = (f32[144,128]{1,0:T(8,128)}, f32[144,128]{1,0:T(8,128)S(1)}, u32[]{:S(2)}) copy-start(f32[144,128]{1,0:T(8,128)S(1)} %add_add_fusion.refs_1_) | copy-start | bytes 221188
  406.5 5.5 %collective-permute-start.9 = (f32[144,128]{1,0:T(8,128)S(1)}, f32[144,128]{1,0:T(8,128)S(1)}, u32[]{:S(2)}, u32[]{:S(2)}) collective-permute-start(f32[144,128]{1,0:T(8,128)S(1)} %add_add_fusion.refs_1_), channel_id=1, source_target_pairs={{0,6},{1,7},{2,4},{3,5},{4,2},{5,3},{6,0},{7,1},{8,14},{9,15},{10,... | collective-permute-start | bytes 221192 | tf_op jit(solution)/shard_map/ppermute | solution.py:358
  407.5 5.1 %collective-permute-start.8 = (f32[144,128]{1,0:T(8,128)S(1)}, f32[144,128]{1,0:T(8,128)S(1)}, u32[]{:S(2)}, u32[]{:S(2)}) collective-permute-start(f32[144,128]{1,0:T(8,128)S(1)} %add_add_fusion.refs_1_), channel_id=1, source_target_pairs={{0,4},{1,5},{2,6},{3,7},{4,0},{5,1},{6,2},{7,3},{8,12},{9,13},{10,... | collective-permute-start | bytes 221192 | tf_op jit(solution)/shard_map/ppermute | solution.py:358
  408.8 4.4 %collective-permute-start.7 = (f32[144,128]{1,0:T(8,128)S(1)}, f32[144,128]{1,0:T(8,128)S(1)}, u32[]{:S(2)}, u32[]{:S(2)}) collective-permute-start(f32[144,128]{1,0:T(8,128)S(1)} %add_add_fusion.refs_1_), channel_id=1, source_target_pairs={{0,2},{1,3},{2,0},{3,1},{4,6},{5,7},{6,4},{7,5},{8,10},{9,11},{10,... | collective-permute-start | bytes 221192 | tf_op jit(solution)/shard_map/ppermute | solution.py:358
  410.0 3.2 collective-permute-start.10
  412.0 2.4 copy-start.1
  412.0 1.3 collective-permute-start.13
  412.7 1.7 copy-start.2
  412.7 1.3 collective-permute-start.12
  413.1 1.3 copy-start.3
  413.1 1.3 collective-permute-start.11
  413.2 1.2 copy-start.4
  413.3 1.2 copy-start.5
  413.9 0.6 copy-start.6
  414.4 0.6 copy-start.7

commit v7 on v6

--- a/solution.py
+++ b/solution.py
@@ -68,14 +68,17 @@
     for n, size in enumerate(piece_sizes(block_ref.shape[1])):
         view = (slice(None), pl.ds(first, size))
         copy = pltpu.make_async_copy(block_ref.at[view], held_ref.at[view], sems.at[n])
-        copy.start()
         arrivals.append((copy, view))
         first += size
+    for copy, _ in arrivals[:2]:
+        copy.start()
     rows, group = parts[0].shape
     planes_total = total_ref.shape[0]
     half = planes_total // 2 // group * group
     for n, (copy, view) in enumerate(arrivals):
         copy.wait()
+        if n + 2 < len(arrivals):
+            arrivals[n + 2][0].start()
         high, low = split(cell_matrix(held_ref.at[view]))
         mixed = nt(high, low * jnp.bfloat16(2))
         total_ref[...] = mixed if n == 0 else total_ref[...] + mixed

time: 429 us -> 429 us (level)
  no operation moved by 1% of the time
where the time goes in v7:
time: 429 us
  blocking collectives  371 us (86%)
  Pallas kernels  31 us (7%)
  waiting for transfers between devices  14.5 us (3%)
  starting transfers between devices  11.7 us (3%)
    all_to_all x1, blocking collectives, local(): lax.all_to_all(outgoing(velocity), ('ta', 'af'), split_axis=0, concat_axi...  371 us
    pallas_call x1, Pallas kernels, finish(): pl.pallas_call(functools.partial(finish_kernel, len(pieces), len(blocks))...  13.4 us
    pallas_call x1, Pallas kernels, gram_pack(): pl.pallas_call(gram_pack_kernel, in_specs=[pl.BlockSpec(memory_space=pl.A...  11.4 us
  transfers between devices with their start and end apart: 14, of which 12 were waited for; matrix products, arithmetic and copies ran while one was open for 0% of the time, Pallas kernels for 0%

profile of v7, /device:TPU:0, one launch (start us, length us, event | category | flops | bytes accessed | tf_op | source)
XLA Modules:
  0.0 428.6 jit_solution(17858866063073269567)
XLA Ops:
  0.0 6.1 %arrange.1 = f32[32,64,16,128]{3,2,1,0:T(8,128)S(1)} custom-call(f32[16,16,8,16,128]{4,3,2,1,0:T(8,128)} %bitcast.3), custom_call_target="tpu_custom_call" | custom-call | tf_op jit(solution)/shard_map/arrange/pallas_call | solution.py:415
  6.1 370.5 %all_to_all.5.block_ref.refs_9_ = f32[32,64,16,128]{3,2,1,0:T(8,128)} all-to-all(f32[32,64,16,128]{3,2,1,0:T(8,128)S(1)} %arrange.1), channel_id=1, replica_groups=mesh['ta'=4,'af'=8] {'ta','af'}, dimensions={0} | all-to-all | bytes 33554432 | tf_op jit(solution)/shard_map/all_to_all | solution.py:435
  376.6 11.4 %gram_pack.1 = (f32[576,128]{1,0:T(8,128)S(1)}, f32[576,128]{1,0:T(8,128)S(1)}) custom-call(f32[32,64,16,128]{3,2,1,0:T(8,128)} %all_to_all.5.block_ref.refs_9_), custom_call_target="tpu_custom_call" | custom-call | tf_op jit(solution)/shard_map/gram_pack/pallas_call | solution.py:137
  388.1 1.6 collective-permute-done.came_ref
  389.7 1.8 collective-permute-start.1
  391.5 1.3 collective-permute-start.2
  392.8 0.5 collective-permute-start.3
  393.3 0.9 collective-permute-done.1
  394.2 1.7 collective-permute-done.2
  395.9 2.1 collective-permute-done.3
  398.0 2.1 collective-permute-start.6
  400.1 2.4 collective-permute-start.4
  402.5 2.1 collective-permute-done.6
  404.6 1.9 collective-permute-done.5
  406.5 1.0 collective-permute-start.9
  407.5 1.2 collective-permute-start.8
  408.8 1.3 collective-permute-start.7
  410.0 1.9 collective-permute-done.9.refs_4_
  412.0 0.7 collective-permute-done.8.refs_3_
  412.7 0.4 collective-permute-done.7.refs_2_
  413.3 0.7 collective-permute-done.12.refs_7_
  413.9 0.4 collective-permute-done.11.refs_6_
  414.6 0.4 copy-done.7
  415.0 13.4 %finish.1 = f32[64,64,128]{2,1,0:T(8,128)} custom-call(f32[64,512]{1,0:T(8,128)} %bitcast.4, f32[144,128]{1,0:T(8,128)} %copy-done, f32[144,128]{1,0:T(8,128)} %copy-done.3, f32[144,128]{1,0:T(8,128)} %copy-done.2, f32[144,128]{1,0:T(8,128)} %copy-done.1, f32[144,128]{1,0:T(8,128)} %copy-done.4, f32[144,128]{1,0:T(8,128)} %copy-done.7, ...), custom_call_target="tpu_custom_call" | custom-call | tf_op jit(solution)/shard_map/finish/pallas_call | solution.py:283
  (27 shorter events, 0.5 us)
Async XLA Ops:
  388.0 1.6 collective-permute-start
  389.7 4.4 %collective-permute-start.1 = (f32[144,128]{1,0:T(8,128)S(1)}, f32[144,128]{1,0:T(8,128)S(1)}, u32[]{:S(2)}, u32[]{:S(2)}) collective-permute-start(f32[144,128]{1,0:T(8,128)S(1)} %get-tuple-element.14), channel_id=1, source_target_pairs={{0,2},{1,3},{2,0},{3,1},{4,6},{5,7},{6,4},{7,5},{8,10},{9,11},{10,... | collective-permute-start | bytes 221192 | tf_op jit(solution)/shard_map/ppermute | solution.py:361
  391.5 4.4 %collective-permute-start.2 = (f32[144,128]{1,0:T(8,128)S(1)}, f32[144,128]{1,0:T(8,128)S(1)}, u32[]{:S(2)}, u32[]{:S(2)}) collective-permute-start(f32[144,128]{1,0:T(8,128)S(1)} %get-tuple-element.15), channel_id=1, source_target_pairs={{0,4},{1,5},{2,6},{3,7},{4,0},{5,1},{6,2},{7,3},{8,12},{9,13},{10,... | collective-permute-start | bytes 221192 | tf_op jit(solution)/shard_map/ppermute | solution.py:361
  392.8 5.3 %collective-permute-start.3 = (f32[144,128]{1,0:T(8,128)S(1)}, f32[144,128]{1,0:T(8,128)S(1)}, u32[]{:S(2)}, u32[]{:S(2)}) collective-permute-start(f32[144,128]{1,0:T(8,128)S(1)} %get-tuple-element.16), channel_id=1, source_target_pairs={{0,6},{1,7},{2,4},{3,5},{4,2},{5,3},{6,0},{7,1},{8,14},{9,15},{10,... | collective-permute-start | bytes 221192 | tf_op jit(solution)/shard_map/ppermute | solution.py:361
  398.0 6.5 %collective-permute-start.6 = (f32[144,128]{1,0:T(8,128)S(1)}, f32[144,128]{1,0:T(8,128)S(1)}, u32[]{:S(2)}, u32[]{:S(2)}) collective-permute-start(f32[144,128]{1,0:T(8,128)S(1)} %add_add_fusion.1), channel_id=1, source_target_pairs={{0,24},{8,16},{16,8},{24,0},{1,25},{9,17},{17,9},{25,1},{2,26},{10... | collective-permute-start | bytes 221192 | tf_op jit(solution)/shard_map/ppermute | solution.py:368
  400.1 6.3 %collective-permute-start.5 = (f32[144,128]{1,0:T(8,128)S(1)}, f32[144,128]{1,0:T(8,128)S(1)}, u32[]{:S(2)}, u32[]{:S(2)}) collective-permute-start(f32[144,128]{1,0:T(8,128)S(1)} %add_add_fusion.1), channel_id=1, source_target_pairs={{0,16},{8,24},{16,0},{24,8},{1,17},{9,25},{17,1},{25,9},{2,18},{10... | collective-permute-start | bytes 221192 | tf_op jit(solution)/shard_map/ppermute | solution.py:368
  400.1 6.3 %collective-permute-start.4 = (f32[144,128]{1,0:T(8,128)S(1)}, f32[144,128]{1,0:T(8,128)S(1)}, u32[]{:S(2)}, u32[]{:S(2)}) collective-permute-start(f32[144,128]{1,0:T(8,128)S(1)} %add_add_fusion.1), channel_id=1, source_target_pairs={{0,8},{8,0},{16,24},{24,16},{1,9},{9,1},{17,25},{25,17},{2,10},{10... | collective-permute-start | bytes 221192 | tf_op jit(solution)/shard_map/ppermute | solution.py:368
  406.5 7.9 %copy-start = (f32[144,128]{1,0:T(8,128)}, f32[144,128]{1,0:T(8,128)S(1)}, u32[]{:S(2)}) copy-start(f32[144,128]{1,0:T(8,128)S(1)} %add_add_fusion.refs_1_) | copy-start | bytes 221188
  406.5 5.5 %collective-permute-start.9 = (f32[144,128]{1,0:T(8,128)S(1)}, f32[144,128]{1,0:T(8,128)S(1)}, u32[]{:S(2)}, u32[]{:S(2)}) collective-permute-start(f32[144,128]{1,0:T(8,128)S(1)} %add_add_fusion.refs_1_), channel_id=1, source_target_pairs={{0,6},{1,7},{2,4},{3,5},{4,2},{5,3},{6,0},{7,1},{8,14},{9,15},{10,... | collective-permute-start | bytes 221192 | tf_op jit(solution)/shard_map/ppermute | solution.py:361
  407.5 5.1 %collective-permute-start.8 = (f32[144,128]{1,0:T(8,128)S(1)}, f32[144,128]{1,0:T(8,128)S(1)}, u32[]{:S(2)}, u32[]{:S(2)}) collective-permute-start(f32[144,128]{1,0:T(8,128)S(1)} %add_add_fusion.refs_1_), channel_id=1, source_target_pairs={{0,4},{1,5},{2,6},{3,7},{4,0},{5,1},{6,2},{7,3},{8,12},{9,13},{10,... | collective-permute-start | bytes 221192 | tf_op jit(solution)/shard_map/ppermute | solution.py:361
  408.8 4.4 %collective-permute-start.7 = (f32[144,128]{1,0:T(8,128)S(1)}, f32[144,128]{1,0:T(8,128)S(1)}, u32[]{:S(2)}, u32[]{:S(2)}) collective-permute-start(f32[144,128]{1,0:T(8,128)S(1)} %add_add_fusion.refs_1_), channel_id=1, source_target_pairs={{0,2},{1,3},{2,0},{3,1},{4,6},{5,7},{6,4},{7,5},{8,10},{9,11},{10,... | collective-permute-start | bytes 221192 | tf_op jit(solution)/shard_map/ppermute | solution.py:361
  410.0 3.1 collective-permute-start.10
  412.0 2.4 copy-start.1
  412.0 1.3 collective-permute-start.13
  412.7 1.7 copy-start.2
  412.7 1.3 collective-permute-start.12
  413.1 1.3 copy-start.3
  413.1 1.3 collective-permute-start.11
  413.2 1.2 copy-start.4
  413.3 1.2 copy-start.5
  413.9 0.6 copy-start.6
  414.4 0.6 copy-start.7

commit v8 on v6

--- a/solution.py
+++ b/solution.py
@@ -11,7 +11,7 @@
 HIGHEST = lax.Precision.HIGHEST
 MIB = 1024 * 1024
 PIVOTS = 16
-PROJECT_CELLS = 8
+PROJECT_CELLS = 16
 
 
 def split(matrix):

time: 429 us -> 429 us (level)
  no operation moved by 1% of the time
where the time goes in v8:
time: 429 us; the launch traced here: 428 us
  blocking collectives  371 us (86%)
  Pallas kernels  30.8 us (7%)
  waiting for transfers between devices  14.5 us (3%)
  starting transfers between devices  11.7 us (3%)
    all_to_all x1, blocking collectives, local(): lax.all_to_all(outgoing(velocity), ('ta', 'af'), split_axis=0, concat_axi...  371 us
    pallas_call x1, Pallas kernels, finish(): pl.pallas_call(functools.partial(finish_kernel, len(pieces), len(blocks))...  13.2 us
    pallas_call x1, Pallas kernels, gram_pack(): pl.pallas_call(gram_pack_kernel, in_specs=[pl.BlockSpec(memory_space=pl.A...  11.4 us
  transfers between devices with their start and end apart: 14, of which 12 were waited for; matrix products, arithmetic and copies ran while one was open for 0% of the time, Pallas kernels for 0%

profile of v8, /device:TPU:0, one launch (start us, length us, event | category | flops | bytes accessed | tf_op | source)
XLA Modules:
  0.0 428.4 jit_solution(10170164313638599982)
XLA Ops:
  0.0 6.1 %arrange.1 = f32[32,64,16,128]{3,2,1,0:T(8,128)S(1)} custom-call(f32[16,16,8,16,128]{4,3,2,1,0:T(8,128)} %bitcast.3), custom_call_target="tpu_custom_call" | custom-call | tf_op jit(solution)/shard_map/arrange/pallas_call | solution.py:412
  6.1 370.5 %all_to_all.5.block_ref.refs_9_ = f32[32,64,16,128]{3,2,1,0:T(8,128)} all-to-all(f32[32,64,16,128]{3,2,1,0:T(8,128)S(1)} %arrange.1), channel_id=1, replica_groups=mesh['ta'=4,'af'=8] {'ta','af'}, dimensions={0} | all-to-all | bytes 33554432 | tf_op jit(solution)/shard_map/all_to_all | solution.py:432
  376.6 11.4 %gram_pack.1 = (f32[576,128]{1,0:T(8,128)S(1)}, f32[576,128]{1,0:T(8,128)S(1)}) custom-call(f32[32,64,16,128]{3,2,1,0:T(8,128)} %all_to_all.5.block_ref.refs_9_), custom_call_target="tpu_custom_call" | custom-call | tf_op jit(solution)/shard_map/gram_pack/pallas_call | solution.py:134
  388.1 1.6 collective-permute-done.came_ref
  389.7 1.8 collective-permute-start.1
  391.5 1.3 collective-permute-start.2
  392.8 0.5 collective-permute-start.3
  393.3 0.9 collective-permute-done.1
  394.2 1.7 collective-permute-done.2
  395.9 2.1 collective-permute-done.3
  398.0 2.1 collective-permute-start.6
  400.1 2.4 collective-permute-start.4
  402.5 2.1 collective-permute-done.6
  404.6 1.8 collective-permute-done.5
  406.5 1.1 collective-permute-start.9
  407.5 1.2 collective-permute-start.8
  408.8 1.3 collective-permute-start.7
  410.0 1.9 collective-permute-done.9.refs_4_
  412.0 0.7 collective-permute-done.8.refs_3_
  412.7 0.4 collective-permute-done.7.refs_2_
  413.3 0.7 collective-permute-done.12.refs_7_
  413.9 0.4 collective-permute-done.11.refs_6_
  414.6 0.4 copy-done.7
  415.0 13.2 %finish.1 = f32[64,64,128]{2,1,0:T(8,128)} custom-call(f32[64,512]{1,0:T(8,128)} %bitcast.4, f32[144,128]{1,0:T(8,128)} %copy-done, f32[144,128]{1,0:T(8,128)} %copy-done.3, f32[144,128]{1,0:T(8,128)} %copy-done.2, f32[144,128]{1,0:T(8,128)} %copy-done.1, f32[144,128]{1,0:T(8,128)} %copy-done.4, f32[144,128]{1,0:T(8,128)} %copy-done.7, ...), custom_call_target="tpu_custom_call" | custom-call | tf_op jit(solution)/shard_map/finish/pallas_call | solution.py:280
  (27 shorter events, 0.5 us)
Async XLA Ops:
  388.0 1.6 collective-permute-start
  389.7 4.4 %collective-permute-start.1 = (f32[144,128]{1,0:T(8,128)S(1)}, f32[144,128]{1,0:T(8,128)S(1)}, u32[]{:S(2)}, u32[]{:S(2)}) collective-permute-start(f32[144,128]{1,0:T(8,128)S(1)} %get-tuple-element.14), channel_id=1, source_target_pairs={{0,2},{1,3},{2,0},{3,1},{4,6},{5,7},{6,4},{7,5},{8,10},{9,11},{10,... | collective-permute-start | bytes 221192 | tf_op jit(solution)/shard_map/ppermute | solution.py:358
  391.5 4.4 %collective-permute-start.2 = (f32[144,128]{1,0:T(8,128)S(1)}, f32[144,128]{1,0:T(8,128)S(1)}, u32[]{:S(2)}, u32[]{:S(2)}) collective-permute-start(f32[144,128]{1,0:T(8,128)S(1)} %get-tuple-element.15), channel_id=1, source_target_pairs={{0,4},{1,5},{2,6},{3,7},{4,0},{5,1},{6,2},{7,3},{8,12},{9,13},{10,... | collective-permute-start | bytes 221192 | tf_op jit(solution)/shard_map/ppermute | solution.py:358
  392.8 5.3 %collective-permute-start.3 = (f32[144,128]{1,0:T(8,128)S(1)}, f32[144,128]{1,0:T(8,128)S(1)}, u32[]{:S(2)}, u32[]{:S(2)}) collective-permute-start(f32[144,128]{1,0:T(8,128)S(1)} %get-tuple-element.16), channel_id=1, source_target_pairs={{0,6},{1,7},{2,4},{3,5},{4,2},{5,3},{6,0},{7,1},{8,14},{9,15},{10,... | collective-permute-start | bytes 221192 | tf_op jit(solution)/shard_map/ppermute | solution.py:358
  398.0 6.6 %collective-permute-start.6 = (f32[144,128]{1,0:T(8,128)S(1)}, f32[144,128]{1,0:T(8,128)S(1)}, u32[]{:S(2)}, u32[]{:S(2)}) collective-permute-start(f32[144,128]{1,0:T(8,128)S(1)} %add_add_fusion.1), channel_id=1, source_target_pairs={{0,24},{8,16},{16,8},{24,0},{1,25},{9,17},{17,9},{25,1},{2,26},{10... | collective-permute-start | bytes 221192 | tf_op jit(solution)/shard_map/ppermute | solution.py:365
  400.1 6.3 %collective-permute-start.5 = (f32[144,128]{1,0:T(8,128)S(1)}, f32[144,128]{1,0:T(8,128)S(1)}, u32[]{:S(2)}, u32[]{:S(2)}) collective-permute-start(f32[144,128]{1,0:T(8,128)S(1)} %add_add_fusion.1), channel_id=1, source_target_pairs={{0,16},{8,24},{16,0},{24,8},{1,17},{9,25},{17,1},{25,9},{2,18},{10... | collective-permute-start | bytes 221192 | tf_op jit(solution)/shard_map/ppermute | solution.py:365
  400.1 6.3 %collective-permute-start.4 = (f32[144,128]{1,0:T(8,128)S(1)}, f32[144,128]{1,0:T(8,128)S(1)}, u32[]{:S(2)}, u32[]{:S(2)}) collective-permute-start(f32[144,128]{1,0:T(8,128)S(1)} %add_add_fusion.1), channel_id=1, source_target_pairs={{0,8},{8,0},{16,24},{24,16},{1,9},{9,1},{17,25},{25,17},{2,10},{10... | collective-permute-start | bytes 221192 | tf_op jit(solution)/shard_map/ppermute | solution.py:365
  406.5 7.9 %copy-start = (f32[144,128]{1,0:T(8,128)}, f32[144,128]{1,0:T(8,128)S(1)}, u32[]{:S(2)}) copy-start(f32[144,128]{1,0:T(8,128)S(1)} %add_add_fusion.refs_1_) | copy-start | bytes 221188
  406.5 5.5 %collective-permute-start.9 = (f32[144,128]{1,0:T(8,128)S(1)}, f32[144,128]{1,0:T(8,128)S(1)}, u32[]{:S(2)}, u32[]{:S(2)}) collective-permute-start(f32[144,128]{1,0:T(8,128)S(1)} %add_add_fusion.refs_1_), channel_id=1, source_target_pairs={{0,6},{1,7},{2,4},{3,5},{4,2},{5,3},{6,0},{7,1},{8,14},{9,15},{10,... | collective-permute-start | bytes 221192 | tf_op jit(solution)/shard_map/ppermute | solution.py:358
  407.5 5.1 %collective-permute-start.8 = (f32[144,128]{1,0:T(8,128)S(1)}, f32[144,128]{1,0:T(8,128)S(1)}, u32[]{:S(2)}, u32[]{:S(2)}) collective-permute-start(f32[144,128]{1,0:T(8,128)S(1)} %add_add_fusion.refs_1_), channel_id=1, source_target_pairs={{0,4},{1,5},{2,6},{3,7},{4,0},{5,1},{6,2},{7,3},{8,12},{9,13},{10,... | collective-permute-start | bytes 221192 | tf_op jit(solution)/shard_map/ppermute | solution.py:358
  408.8 4.4 %collective-permute-start.7 = (f32[144,128]{1,0:T(8,128)S(1)}, f32[144,128]{1,0:T(8,128)S(1)}, u32[]{:S(2)}, u32[]{:S(2)}) collective-permute-start(f32[144,128]{1,0:T(8,128)S(1)} %add_add_fusion.refs_1_), channel_id=1, source_target_pairs={{0,2},{1,3},{2,0},{3,1},{4,6},{5,7},{6,4},{7,5},{8,10},{9,11},{10,... | collective-permute-start | bytes 221192 | tf_op jit(solution)/shard_map/ppermute | solution.py:358
  410.0 3.2 collective-permute-start.10
  412.0 2.4 copy-start.1
  412.0 1.3 collective-permute-start.13
  412.7 1.7 copy-start.2
  412.7 1.3 collective-permute-start.12
  413.1 1.3 copy-start.3
  413.1 1.3 collective-permute-start.11
  413.2 1.2 copy-start.4
  413.3 1.2 copy-start.5
  413.9 0.6 copy-start.6
  414.4 0.6 copy-start.7
